TPU v7x, 256 devices: a whole 4x4x8 slice. The times are simulated.
256 devices in a mesh: depth: 8 (over y_lo, x), row: 4 (over y_hi, core), col: 8 (over z).
Axes of the slice: x: 4, y: 4 (y_hi: 2, y_lo: 2; y = y_hi * 2 + y_lo), z: 8, core: 2. Of those that a mesh axis runs over, the one named last changes fastest.
Arguments:
- tokens: bfloat16 [4096, 3072], P('depth', 'row'), may hold values from -6 to 6
- gate_weight: bfloat16 [3072, 16384], P('row', 'col'), may hold values from -0.109375 to 0.109375
- up_weight: bfloat16 [3072, 16384], P('row', 'col'), may hold values from -0.109375 to 0.109375
- down_weight: bfloat16 [16384, 3072], P('col', 'row'), may hold values from -0.046875 to 0.046875
- output_grad: bfloat16 [4096, 3072], P('depth', 'row'), may hold values from -6 to 6
Outputs:
- mlp_output: bfloat16 [4096, 3072], P('depth', 'row')
- input_grad: bfloat16 [4096, 3072], P('depth', 'row')
- gate_weight_grad: float32 [8, 3072, 2048], P('depth', 'row', 'col')
- up_weight_grad: float32 [8, 3072, 2048], P('depth', 'row', 'col')
- down_weight_grad: float32 [8, 2048, 3072], P('depth', 'col', 'row')
All inputs are finite; a program needn't handle non-finite values.
Results may differ from a plain program's by a relative error of at most 0.005.
Values may be sent and summed in bfloat16 or wider, within the bound.
No kernel may reach another device: no remote copies, remote signals or barrier semaphores. Data moves between devices by JAX's collectives and lax.ppermute only.
A program may use at most 128 MiB of HBM per device.

v0:
```python
import jax
import jax.numpy as jnp
from jax import lax
from jax.sharding import PartitionSpec as P

grad_scale = 0.03125


def contract(left_array, right_array, left_axis, right_axis):
    return lax.dot_general(
        left_array,
        right_array,
        (((left_axis,), (right_axis,)), ((), ())),
        preferred_element_type=jnp.float32,
    )


def local(tokens, gate_weight, up_weight, down_weight, output_grad):
    hidden_width = gate_weight.shape[1]
    row_block = tokens
    gate_up = lax.psum_scatter(
        jnp.concatenate(
            [
                jnp.dot(row_block, gate_weight, preferred_element_type=jnp.float32),
                jnp.dot(row_block, up_weight, preferred_element_type=jnp.float32),
            ],
            axis=1,
        ),
        "row",
        scatter_dimension=0,
        tiled=True,
    )
    gate_values = gate_up[:, :hidden_width]
    up_values = gate_up[:, hidden_width:]
    sigmoid_values = jax.nn.sigmoid(gate_values)
    silu_values = gate_values * sigmoid_values
    hidden = (silu_values * up_values).astype(jnp.bfloat16)
    hidden_whole = lax.all_gather(hidden, "row", axis=0, tiled=True)
    partial_value = jnp.dot(hidden_whole, down_weight, preferred_element_type=jnp.float32)
    mlp_output = lax.psum(partial_value, "col").astype(jnp.bfloat16)
    row_block = output_grad
    hidden_grad = lax.psum_scatter(
        contract(row_block, down_weight, 1, 1), "row", scatter_dimension=0, tiled=True
    )
    gate_grad = (
        hidden_grad * up_values * sigmoid_values * (1.0 + gate_values * (1.0 - sigmoid_values))
    ).astype(jnp.bfloat16)
    up_grad = (hidden_grad * silu_values).astype(jnp.bfloat16)
    grad_whole = lax.all_gather(jnp.stack([gate_grad, up_grad], axis=1), "row", axis=0, tiled=True)
    input_part = contract(grad_whole[:, 0], gate_weight, 1, 1) + contract(
        grad_whole[:, 1], up_weight, 1, 1
    )
    input_grad = lax.psum(input_part, "col").astype(jnp.bfloat16)
    gate_local = contract(tokens, grad_whole[:, 0], 0, 0)
    up_local = contract(tokens, grad_whole[:, 1], 0, 0)
    gate_sum, up_sum = (
        lax.psum_scatter(gate_local, "depth", scatter_dimension=1, tiled=True),
        lax.psum_scatter(up_local, "depth", scatter_dimension=1, tiled=True),
    )
    down_sum = lax.psum_scatter(
        contract(hidden_whole, output_grad, 0, 0), "depth", scatter_dimension=0, tiled=True
    )
    return (
        mlp_output,
        input_grad,
        (gate_sum * grad_scale)[None],
        (up_sum * grad_scale)[None],
        (down_sum * grad_scale)[None],
    )


def solution(mesh):
    placed = (
        P("depth", "row"),
        P("row", "col"),
        P("row", "col"),
        P("col", "row"),
        P("depth", "row"),
    )
    return jax.shard_map(
        local,
        mesh=mesh,
        in_specs=placed,
        out_specs=(
            P("depth", "row"),
            P("depth", "row"),
            P("depth", "row", "col"),
            P("depth", "row", "col"),
            P("depth", "col", "row"),
        ),
        check_vma=False,
    )
```

profile of v0, /device:TPU:1, one launch (start us, length us, event | category | flops | bytes accessed | tf_op | source)
XLA Modules:
  0.0 477.5 jit_solution(4719091944618979433)
XLA Ops:
  7.2 1.8 copy-done
  9.1 4.9 %fusion.9 = f32[512,2048]{1,0:T(8,128)} fusion(bf16[512,768]{1,0:T(8,128)(2,1)} %param.9, bf16[2048,768]{1,0:T(8,128)(2,1)S(1)} %copy-done), kind=kOutput, calls=%fused_computation.22 | convolution fusion | flops 1610612736 | bytes 8126464 | tf_op jit(solution)/shard_map/dot_general | solution.py:10
  14.0 0.0 reduce-scatter.6.cloned.1.call-start
  14.1 4.1 fusion.6
  18.2 1.8 fusion.7
  20.0 3.8 pad_maximum_fusion
  23.8 0.0 all-gather.3.cloned.1.call-start
  23.8 50.7 %reduce-scatter.8.cloned.1.call-done = f32[128,2048]{1,0:T(8,128)} async-done(((f32[512,2048]{1,0:T(8,128)}), f32[128,2048]{1,0:T(8,128)}) %reduce-scatter.8.cloned.1.call-update) | async-done | bytes 1048592 | tf_op jit(solution)/shard_map/reduce_scatter | solution.py:42
  74.5 86.3 %reduce-scatter.6.cloned.1.call-done = f32[128,4096]{1,0:T(8,128)} async-done(((f32[512,4096]{1,0:T(8,128)}), f32[128,4096]{1,0:T(8,128)}) %reduce-scatter.6.cloned.1.call-update) | async-done | bytes 2097168 | tf_op jit(solution)/shard_map/reduce_scatter | solution.py:21
  160.9 3.6 fusion.5
  164.5 0.0 all-gather.5.cloned.1.call-start
  164.5 2.3 pad_maximum_fusion.1
  166.9 0.0 reduce-scatter.14.cloned.1.call-start
  166.9 26.8 %all-gather.3.cloned.1.call-done = bf16[512,2048]{1,0:T(8,128)(2,1)} async-done(((bf16[128,2048]{1,0:T(8,128)(2,1)}), bf16[512,2048]{1,0:T(8,128)(2,1)}) %all-gather.3.cloned.1.call-update) | async-done | bytes 2097168 | tf_op jit(solution)/shard_map/all_gather | solution.py:38
  193.7 6.3 %fusion.10 = f32[2048,768]{1,0:T(8,128)} fusion(bf16[512,2048]{1,0:T(8,128)(2,1)} %all-gather.3.cloned.1.call-done, bf16[512,768]{1,0:T(8,128)(2,1)} %param.9), kind=kOutput, calls=%fused_computation.23 | convolution fusion | flops 1610612736 | bytes 9175040 | tf_op jit(solution)/shard_map/dot_general | solution.py:10
  200.0 0.0 reduce-scatter.12.cloned.1.call-start
  200.0 35.9 %all-gather.5.cloned.1.call-done = bf16[512,2,2048]{2,0,1:T(8,128)(2,1)} async-done(((bf16[128,2,2048]{2,0,1:T(8,128)(2,1)}), bf16[512,2,2048]{2,0,1:T(8,128)(2,1)}) %all-gather.5.cloned.1.call-update) | async-done | bytes 4194320 | tf_op jit(solution)/shard_map/all_gather | solution.py:49
  235.9 6.2 %convolution_bitcast_fusion = f32[768,2048]{0,1:T(8,128)} fusion(bf16[512,768]{1,0:T(8,128)(2,1)} %param.5, bf16[512,2,2048]{2,0,1:T(8,128)(2,1)} %all-gather.5.cloned.1.call-done), kind=kOutput, calls=%fused_computation.1 | convolution fusion | flops 1610612736 | bytes 9175040 | tf_op jit(solution)/shard_map/dot_general | solution.py:10
  242.1 0.2 reduce-scatter.10.cloned.1.call-start
  242.4 6.3 %convolution_bitcast_fusion.1 = f32[768,2048]{0,1:T(8,128)} fusion(bf16[512,768]{1,0:T(8,128)(2,1)} %param.5, bf16[512,2,2048]{2,0,1:T(8,128)(2,1)} %all-gather.5.cloned.1.call-done), kind=kOutput, calls=%fused_computation.2 | convolution fusion | flops 1610612736 | bytes 9175040 | tf_op jit(solution)/shard_map/dot_general | solution.py:10
  248.7 4.9 %fusion.8 = f32[512,768]{1,0:T(8,128)} fusion(bf16[512,2048]{1,0:T(8,128)(2,1)} %all-gather.3.cloned.1.call-done, bf16[2048,768]{1,0:T(8,128)(2,1)S(1)} %copy-done), kind=kOutput, calls=%fused_computation.21 | convolution fusion | flops 1610612736 | bytes 6815744 | tf_op jit(solution)/shard_map/dot_general | solution.py:39
  253.6 1.8 fusion
  255.4 0.1 copy-done.5
  255.4 3.0 fusion.2
  258.5 67.2 %all-reduce.2 = (bf16[512,768]{1,0:T(8,128)(2,1)}, bf16[512,768]{1,0:T(8,128)(2,1)}) all-reduce(f32[512,768]{1,0:T(8,128)} %fusion.8, f32[512,768]{1,0:T(8,128)} %fusion.2), channel_id=1, replica_groups=mesh['depth'=8,'row'=4,'col'=8] {'col'}, use_global_device_ids=true, to_apply=%region_1.0 | all-reduce | flops 786432 | bytes 4718592 | tf_op jit(solution)/shard_map/psum | solution.py:40
  325.7 2.1 multiply_bitcast_fusion
  327.8 61.7 %reduce-scatter.12.cloned.1.call-done = f32[768,256]{0,1:T(8,128)} async-done(((f32[768,2048]{0,1:T(8,128)}), f32[768,256]{0,1:T(8,128)}) %reduce-scatter.12.cloned.1.call-update) | async-done | bytes 786448 | tf_op jit(solution)/shard_map/reduce_scatter | solution.py:58
  389.5 2.1 multiply_bitcast_fusion.1
  391.6 2.3 copy.11
  393.8 72.5 %reduce-scatter.10.cloned.1.call-done = f32[768,256]{0,1:T(8,128)} async-done(((f32[768,2048]{0,1:T(8,128)}), f32[768,256]{0,1:T(8,128)}) %reduce-scatter.10.cloned.1.call-update) | async-done | bytes 786448 | tf_op jit(solution)/shard_map/reduce_scatter | solution.py:57
  466.3 2.1 multiply_bitcast_fusion.2
  468.4 2.3 copy.10
  (19 shorter events, 0.2 us)
Async XLA Ops:
  7.2 1.9 copy-start
  7.2 67.4 %reduce-scatter.8.cloned.1.call-start = ((), (), s32[]{:S(2)}) async-start(), calls=%async_computation.7 | async-start | bytes 5242880 | tf_op jit(solution)/shard_map/reduce_scatter | solution.py:42
  14.0 146.9 %reduce-scatter.6.cloned.1.call-start = ((), (), s32[]{:S(2)}) async-start(), calls=%async_computation.5 | async-start | bytes 10485760 | tf_op jit(solution)/shard_map/reduce_scatter | solution.py:21
  14.1 4.1 copy-start.2
  14.1 4.1 copy-start.4
  23.8 169.9 %all-gather.3.cloned.1.call-start = ((), (), s32[]{:S(2)}) async-start(), calls=%async_computation.6 | async-start | bytes 2621440 | tf_op jit(solution)/shard_map/all_gather | solution.py:38
  164.5 71.4 %all-gather.5.cloned.1.call-start = ((), (), s32[]{:S(2)}) async-start(), calls=%async_computation.8 | async-start | bytes 5242880 | tf_op jit(solution)/shard_map/all_gather | solution.py:49
  166.9 158.8 %reduce-scatter.14.cloned.1.call-start = ((), (), s32[]{:S(2)}) async-start(), calls=%async_computation.11 | async-start | bytes 7077888 | tf_op jit(solution)/shard_map/reduce_scatter | solution.py:60
  200.0 189.5 %reduce-scatter.12.cloned.1.call-start = ((), (), s32[]{:S(2)}) async-start(), calls=%async_computation.10 | async-start | bytes 7077888 | tf_op jit(solution)/shard_map/reduce_scatter | solution.py:58
  242.1 224.2 %reduce-scatter.10.cloned.1.call-start = ((), (), s32[]{:S(2)}) async-start(), calls=%async_computation.9 | async-start | bytes 7077888 | tf_op jit(solution)/shard_map/reduce_scatter | solution.py:57
  248.6 4.9 %copy-start.1 = (bf16[512,2,2048]{2,0,1:T(8,128)(2,1)S(1)}, bf16[512,2,2048]{2,0,1:T(8,128)(2,1)}, u32[]{:S(2)}) copy-start(bf16[512,2,2048]{2,0,1:T(8,128)(2,1)} %all-gather.5.cloned.1.call-done) | copy-start | bytes 12582916
  248.6 4.9 %copy-start.3 = (bf16[768,2048]{1,0:T(8,128)(2,1)S(1)}, bf16[768,2048]{1,0:T(8,128)(2,1)}, u32[]{:S(2)}) copy-start(bf16[768,2048]{1,0:T(8,128)(2,1)} %param.6) | copy-start | bytes 9437188
  253.6 1.9 copy-start.5
Sparse Core Ops, SparseCore 0:
  14.1 60.3 reduce-scatter.7
  77.6 83.2 reduce-scatter.5
  164.6 29.0 all-gather.2
  195.3 40.5 all-gather.4
  238.3 74.4 reduce-scatter.13
  315.2 74.2 reduce-scatter.11
  392.1 74.2 reduce-scatter.9
where the time goes:
time: 478 us
  waiting for transfers between devices  334 us (70%)
  blocking collectives  67.2 us (14%)
  matrix products  39.2 us (8%)
  other arithmetic  15.9 us (3%)
  between operations  14.2 us (3%)
  local copies, waits for them, and re-layouts  6.48 us (1%)
    reduce_scatter x1, waiting for transfers between devices, local(): lax.psum_scatter(jnp.concatenate([jnp.dot(row_block, gate_weight, preferr...  86.3 us
    reduce_scatter x1, waiting for transfers between devices, local(): lax.psum_scatter(gate_local, 'depth', scatter_dimension=1, tiled=True)  72.5 us
    psum x1, blocking collectives, local(): mlp_output = lax.psum(partial_value, 'col').astype(jnp.bfloat16)  67.2 us
    reduce_scatter x1, waiting for transfers between devices, local(): lax.psum_scatter(up_local, 'depth', scatter_dimension=1, tiled=True)  61.7 us
    reduce_scatter x1, waiting for transfers between devices, local(): lax.psum_scatter(contract(row_block, down_weight, 1, 1), 'row', scatter_d...  50.7 us
    all_gather x1, waiting for transfers between devices, local(): lax.all_gather(jnp.stack([gate_grad, up_grad], axis=1), 'row', axis=0, ti...  35.9 us
    dot_general x6, matrix products, contract(): lax.dot_general(left_array, right_array, (((left_axis,), (right_axis,)),...  28.4 us
    all_gather x1, waiting for transfers between devices, local(): hidden_whole = lax.all_gather(hidden, 'row', axis=0, tiled=True)  26.8 us
  transfers between devices with their start and end apart: 7, of which 6 were waited for; matrix products, arithmetic and copies ran while one was open for 10% of the time, Pallas kernels for 0%

commit v1 on v0

v1 whole, which is shorter than its diff:
```python
import functools

import jax
import jax.numpy as jnp
from jax import lax
from jax.experimental import pallas as pl
from jax.experimental.pallas import tpu as pltpu
from jax.sharding import PartitionSpec as P

grad_scale = 0.03125
wide = 256
n_x = 4
n_col = 8
mib = 1024 * 1024
bf16 = jnp.bfloat16
f32 = jnp.float32

core_swap = [(0, 1), (1, 0), (2, 3), (3, 2)]
half_swap = [(0, 2), (2, 0), (1, 3), (3, 1)]


def x_shift(step):
    return [(y * n_x + x, y * n_x + (x + step) % n_x) for y in range(2) for x in range(n_x)]


def home_swaps():
    first, second = [], []
    for y in range(2):
        for x in range(n_x):
            for half in range(2):
                for core in range(2):
                    at = lambda y_to, core_to: (y_to * n_x + x) * 4 + half * 2 + core_to
                    if core == y:
                        first.append((at(y, core), at(y, 1 - core)))
                    else:
                        first.append((at(y, core), at(1 - y, core)))
                        second.append((at(y, core), at(1 - y, 1 - core)))
    return first, second


home_first, home_second = home_swaps()


def params(limit):
    return pltpu.CompilerParams(vmem_limit_bytes=limit * mib)


def cost(time):
    return pl.CostEstimate(flops=1, bytes_accessed=int(time * 1 * 3.3e6), transcendentals=0)


def mm(left, right):
    return jnp.dot(left, right, preferred_element_type=f32)


def mm_t(left, right):
    return lax.dot_general(left, right, (((1,), (1,)), ((), ())), preferred_element_type=f32)


def after(value, *others):
    return lax.optimization_barrier((value,) + others)[0]


class Chain:
    def __init__(self):
        self.last = None

    def __call__(self, fn, *args):
        if self.last is not None:
            args = (after(args[0], self.last),) + args[1:]
        out = fn(*args)
        self.last = out[0] if isinstance(out, (tuple, list)) else out
        return out


def own_block(step, spot):
    return spot[1] * n_x + lax.rem(spot[0] + step, n_x)


def oth_block(step, spot):
    return lax.rem(spot[0] + step, n_x)


def gate_up_body(spot, own_ref, oth_ref, gate_ref, up_ref, oth_gate_ref, oth_up_ref, out_ref, send_ref):
    for k, (w, oth_w) in enumerate(((gate_ref, oth_gate_ref), (up_ref, oth_up_ref))):
        value = mm(own_ref[...], w[...]) + mm(oth_ref[...], oth_w[...])
        out_ref[:, k * wide : (k + 1) * wide] = value
        send_ref[:, k * wide : (k + 1) * wide] = value.astype(bf16)


def gate_up_partial(steps, spot, own, oth, gate_weight, up_weight, oth_gate, oth_up):
    rows, feat = own.shape
    n = len(steps)
    part = pl.BlockSpec((rows // 2, feat), lambda j, i, s: (i, 0))
    own_w = pl.BlockSpec((feat, wide), lambda j, i, s: (0, own_block(steps[0] + 2 * j, s)))
    oth_w = pl.BlockSpec((feat, wide), lambda j, i, s: (0, oth_block(steps[0] + 2 * j, s)))
    out = pl.BlockSpec((rows // 2, 2 * wide), lambda j, i, s: (i, j))
    return pl.pallas_call(
        gate_up_body,
        grid_spec=pltpu.PrefetchScalarGridSpec(
            num_scalar_prefetch=1,
            grid=(n, 2),
            in_specs=[part, part, own_w, own_w, oth_w, oth_w],
            out_specs=[out, out],
        ),
        out_shape=[
            jax.ShapeDtypeStruct((rows, 2 * wide * n), f32),
            jax.ShapeDtypeStruct((rows, 2 * wide * n), bf16),
        ],
        compiler_params=params(56),
        cost_estimate=cost(4.5),
        name="gate_up_partial",
    )(spot, own, oth, gate_weight, up_weight, oth_gate, oth_up)


def joint_body(gate_up_step, hg_steps, spot, *refs):
    refs = list(refs)
    send_ref, outs = refs[-1], []
    at = 0
    if gate_up_step is not None:
        own_ref, oth_ref, gate_ref, up_ref, oth_gate_ref, oth_up_ref = refs[:6]
        refs = refs[6:]
        out_ref = refs[-2] if not hg_steps else refs[-3]
        for k, (w, oth_w) in enumerate(((gate_ref, oth_gate_ref), (up_ref, oth_up_ref))):
            value = mm(own_ref[...], w[...]) + mm(oth_ref[...], oth_w[...])
            out_ref[:, k * wide : (k + 1) * wide] = value
            send_ref[:, k * wide : (k + 1) * wide] = value.astype(bf16)
        at = 2 * wide
    own_ref, oth_ref = refs[:2]
    out_ref = refs[-2]
    for k in range(len(hg_steps)):
        value = mm_t(own_ref[...], refs[2 + 2 * k][...]) + mm_t(oth_ref[...], refs[3 + 2 * k][...])
        out_ref[:, k * wide : (k + 1) * wide] = value
        send_ref[:, at + k * wide : at + (k + 1) * wide] = value.astype(bf16)


def joint_partial(gate_up_step, hg_steps, spot, tokens_pair, gate_up_weights, grad_pair, down_weights):
    rows, feat = grad_pair[0].shape
    whole = pl.BlockSpec((rows, feat), lambda j, s: (0, 0))
    operands, specs, shapes = [], [], []
    if gate_up_step is not None:
        operands += [*tokens_pair, *gate_up_weights]
        specs += [whole, whole]
        specs += [pl.BlockSpec((feat, wide), lambda j, s: (0, own_block(gate_up_step, s)))] * 2
        specs += [pl.BlockSpec((feat, wide), lambda j, s: (0, oth_block(gate_up_step, s)))] * 2
        shapes.append(jax.ShapeDtypeStruct((rows, 2 * wide), f32))
    operands += [*grad_pair]
    specs += [whole, whole]
    for step in hg_steps:
        operands += [*down_weights]
        specs.append(pl.BlockSpec((wide, feat), lambda j, s, step=step: (own_block(step, s), 0)))
        specs.append(pl.BlockSpec((wide, feat), lambda j, s, step=step: (oth_block(step, s), 0)))
    shapes.append(jax.ShapeDtypeStruct((rows, wide * len(hg_steps)), f32))
    total = sum(shape.shape[1] for shape in shapes)
    shapes.append(jax.ShapeDtypeStruct((rows, total), bf16))
    return pl.pallas_call(
        functools.partial(joint_body, gate_up_step, hg_steps),
        grid_spec=pltpu.PrefetchScalarGridSpec(
            num_scalar_prefetch=1,
            grid=(1,),
            in_specs=specs,
            out_specs=[pl.BlockSpec(shape.shape, lambda j, s: (0, 0)) for shape in shapes],
        ),
        out_shape=shapes,
        compiler_params=params(56),
        cost_estimate=cost(6),
        name="joint_partial",
    )(spot, *operands)


def hidden_body(part_ref, got_ref, hidden_ref, hidden_t_ref):
    gate_up = part_ref[...] + got_ref[...].astype(f32)
    gate_values = gate_up[:, :wide]
    up_values = gate_up[:, wide:]
    silu_values = gate_values * jax.nn.sigmoid(gate_values)
    hidden = (silu_values * up_values).astype(bf16)
    hidden_ref[...] = hidden
    hidden_t_ref[...] = hidden.T


def hidden_step(part, got):
    rows = part.shape[0]
    n = part.shape[1] // (2 * wide)
    pair = pl.BlockSpec((rows, 2 * wide), lambda j: (0, j))
    return pl.pallas_call(
        hidden_body,
        grid=(n,),
        in_specs=[pair, pair],
        out_specs=[
            pl.BlockSpec((rows, wide), lambda j: (0, j)),
            pl.BlockSpec((wide, rows), lambda j: (j, 0)),
        ],
        out_shape=[
            jax.ShapeDtypeStruct((rows, wide * n), bf16),
            jax.ShapeDtypeStruct((wide * n, rows), bf16),
        ],
        compiler_params=params(20),
        cost_estimate=cost(1),
        name="hidden_step",
    )(part, got)


def grads_body(part_ref, got_ref, hg_ref, hg_got_ref, grads_ref):
    gate_up = part_ref[...] + got_ref[...].astype(f32)
    hidden_grad = hg_ref[...] + hg_got_ref[...].astype(f32)
    gate_values = gate_up[:, :wide]
    up_values = gate_up[:, wide:]
    sigmoid_values = jax.nn.sigmoid(gate_values)
    silu_values = gate_values * sigmoid_values
    gate_grad = hidden_grad * up_values * sigmoid_values * (1.0 + gate_values * (1.0 - sigmoid_values))
    up_grad = hidden_grad * silu_values
    grads_ref[:, :wide] = gate_grad.astype(bf16)
    grads_ref[:, wide:] = up_grad.astype(bf16)


def grads_step(hg_at, got_at, part, got, hg, hg_got):
    rows = part.shape[0]
    n = part.shape[1] // (2 * wide)
    pair = pl.BlockSpec((rows, 2 * wide), lambda j: (0, j))
    return pl.pallas_call(
        grads_body,
        grid=(n,),
        in_specs=[
            pair,
            pair,
            pl.BlockSpec((rows, wide), lambda j: (0, hg_at + j)),
            pl.BlockSpec((rows, wide), lambda j: (0, got_at + j)),
        ],
        out_specs=pair,
        out_shape=jax.ShapeDtypeStruct((rows, 2 * wide * n), bf16),
        compiler_params=params(20),
        cost_estimate=cost(1.3),
        name="grads_step",
    )(part, got, hg, hg_got)


def mlp_body(spot, far_ref, near_ref, last_ref, w2, w1, w3, w0, out_ref):
    total = mm(far_ref[...], w2[...]) + mm(near_ref[:, :wide], w1[...])
    total += mm(near_ref[:, wide:], w3[...]) + mm(last_ref[...], w0[...])
    out_ref[...] = total.astype(out_ref.dtype)


def input_body(spot, far_ref, near_ref, last_ref, g2, g1, g3, g0, u2, u1, u3, u0, out_ref):
    total = mm_t(far_ref[:, :wide], g2[...]) + mm_t(far_ref[:, wide:], u2[...])
    total += mm_t(near_ref[:, :wide], g1[...]) + mm_t(near_ref[:, wide : 2 * wide], u1[...])
    total += mm_t(near_ref[:, 2 * wide : 3 * wide], g3[...]) + mm_t(near_ref[:, 3 * wide :], u3[...])
    total += mm_t(last_ref[:, :wide], g0[...]) + mm_t(last_ref[:, wide:], u0[...])
    out_ref[...] = total.astype(out_ref.dtype)


def activation_part(body, block_of, dtype, name, spot, values, weights, by_rows):
    rows = values[0].shape[0]
    feat = weights[0].shape[1 if by_rows else 0]
    whole = [pl.BlockSpec(v.shape, lambda j, s: (0, 0)) for v in values]
    blocks = []
    for _ in weights:
        for step in (2, 1, 3, 0):
            if by_rows:
                blocks.append(pl.BlockSpec((wide, wide), lambda j, s, step=step: (block_of(step, s), j)))
            else:
                blocks.append(pl.BlockSpec((wide, wide), lambda j, s, step=step: (j, block_of(step, s))))
    return pl.pallas_call(
        body,
        grid_spec=pltpu.PrefetchScalarGridSpec(
            num_scalar_prefetch=1,
            grid=(feat // wide,),
            in_specs=whole + blocks,
            out_specs=pl.BlockSpec((rows, wide), lambda j, s: (0, j)),
        ),
        out_shape=jax.ShapeDtypeStruct((rows, feat), dtype),
        compiler_params=params(20),
        cost_estimate=cost(2.5),
        name=name,
    )(spot, *values, *[w for w in weights for _ in range(4)])


def join_body(own_ref, got_ref, out_ref):
    out_ref[...] = (own_ref[...] + got_ref[...].astype(f32)).astype(out_ref.dtype)


def join(dtype, own, got):
    rows, feat = own.shape
    block = pl.BlockSpec((rows // 2, feat), lambda j: (j, 0))
    return pl.pallas_call(
        join_body,
        grid=(2,),
        in_specs=[block, block],
        out_specs=block,
        out_shape=jax.ShapeDtypeStruct(own.shape, dtype),
        compiler_params=params(20),
        cost_estimate=cost(1),
        name="join",
    )(own, got)


def far_body(a0, a1, b0, b1, *out_refs):
    pieces = len(out_refs) // 2
    for a, b, refs in ((a0, b0, out_refs[:pieces]), (a1, b1, out_refs[pieces:])):
        value = mm(a[...], b[...]).astype(bf16)
        n = value.shape[1] // pieces
        for k, ref in enumerate(refs):
            ref[...] = value[:, k * n : (k + 1) * n]


def far_terms(pieces, a, b):
    m, n = a[0].shape[0], b[0].shape[1]
    return pl.pallas_call(
        far_body,
        out_shape=[jax.ShapeDtypeStruct((m, n // pieces), bf16)] * (2 * pieces),
        compiler_params=params(20),
        cost_estimate=cost(1),
        name="far_terms",
    )(*a, *b)


def near_body(a0, a1, c0, c1, b0, b1, d0, d1, *refs):
    pieces = len(refs) // 2 - 1
    rights, lefts = refs[:pieces], refs[pieces : 2 * pieces]
    right_ref, left_ref = refs[-2:]
    m, n = rights[0].shape

    def add(value, got_refs, out_ref, at):
        for k, got in enumerate(got_refs):
            some = value[:, k * n : (k + 1) * n] + got[...].astype(f32)
            out_ref[at : at + m, k * n : (k + 1) * n] = some.astype(bf16)

    add(mm(a0[...], b0[...]), rights, right_ref, 0)
    right_ref[m:, :] = mm(a1[...], b1[...]).astype(bf16)
    left_ref[:m, :] = mm(c0[...], d0[...]).astype(bf16)
    add(mm(c1[...], d1[...]), lefts, left_ref, m)


def window(shape, at):
    return pl.BlockSpec(shape, lambda i: at)


def near_terms(operands, specs, m, n):
    shape = jax.ShapeDtypeStruct((2 * m, n), bf16)
    inner = operands[0].shape[1]
    return pl.pallas_call(
        near_body,
        grid=(1,),
        in_specs=specs,
        out_specs=[window(shape.shape, (0, 0))] * 2,
        out_shape=[shape, shape],
        compiler_params=params(20),
        cost_estimate=cost(2.2),
        name="near_terms",
    )(*operands)


def last_body(spot, a0, a1, b0, b1, from_left, from_right, keep_ref, first_ref, second_ref):
    m = keep_ref.shape[0]
    own = mm(a0[...], b0[...]) + from_left[:m, :].astype(f32) + from_right[:m, :].astype(f32)
    oth = mm(a1[...], b1[...]) + from_left[m:, :].astype(f32) + from_right[m:, :].astype(f32)
    keep_ref[...] = own
    second_ref[...] = oth.astype(bf16)

    @pl.when(spot[3] == 1)
    def _():
        first_ref[...] = oth.astype(bf16)

    @pl.when(spot[3] == 0)
    def _():
        first_ref[...] = own.astype(bf16)


def last_terms(spot, operands, specs, m, n):
    inner = operands[0].shape[1]
    block = pl.BlockSpec((m, n), lambda i, s: (0, 0))
    return pl.pallas_call(
        last_body,
        grid_spec=pltpu.PrefetchScalarGridSpec(
            num_scalar_prefetch=1,
            grid=(1,),
            in_specs=[pl.BlockSpec(shape, lambda i, s, at=at: at) for shape, at in specs],
            out_specs=[block, block, block],
        ),
        out_shape=[
            jax.ShapeDtypeStruct((m, n), f32),
            jax.ShapeDtypeStruct((m, n), bf16),
            jax.ShapeDtypeStruct((m, n), bf16),
        ],
        compiler_params=params(20),
        cost_estimate=cost(1.3),
        name="last_terms",
    )(spot, *operands)


def collect_body(mlp_ref, parts_ref, out_ref):
    height, feat = mlp_ref.shape
    total = parts_ref[:height, :].astype(f32)
    for j in range(1, n_col):
        total = total + parts_ref[j * height : (j + 1) * height, :].astype(f32)
    out_ref[:, :feat] = mlp_ref[...].astype(bf16)
    out_ref[:, feat:] = total.astype(bf16)


def collect(mlp_sum, parts):
    height, feat = mlp_sum.shape
    return pl.pallas_call(
        collect_body,
        out_shape=jax.ShapeDtypeStruct((height, 2 * feat), bf16),
        compiler_params=params(20),
        cost_estimate=cost(1),
        name="collect",
    )(mlp_sum, parts)


def finish_body(spot, one_ref, keep_ref, two_ref, *out_refs):
    one = one_ref[...].astype(f32)
    n = out_refs[0].shape[2]

    def store(value):
        for k, out_ref in enumerate(out_refs):
            out_ref[0] = value[:, k * n : (k + 1) * n]

    @pl.when(spot[3] == 1)
    def _():
        store((keep_ref[...] + one) * grad_scale)

    @pl.when(spot[3] == 0)
    def _():
        store((two_ref[...].astype(f32) + one) * grad_scale)


def finish(outs, spot, one, keep, two):
    m, n = one.shape
    block = pl.BlockSpec((m, n), lambda i, s: (0, 0))
    shape = jax.ShapeDtypeStruct((1, m, n // outs), f32)
    return pl.pallas_call(
        finish_body,
        grid_spec=pltpu.PrefetchScalarGridSpec(
            num_scalar_prefetch=1,
            grid=(1,),
            in_specs=[block] * 3,
            out_specs=[pl.BlockSpec(shape.shape, lambda i, s: (0, 0, 0))] * outs,
        ),
        out_shape=[shape] * outs,
        compiler_params=params(20),
        cost_estimate=cost(1.5),
        name="finish",
    )(spot, one, keep, two)


def local(tokens, gate_weight, up_weight, down_weight, output_grad):
    rows, feat = tokens.shape
    depth_id = lax.axis_index("depth")
    x_id = depth_id % n_x
    y_lo = depth_id // n_x
    core = lax.axis_index("row") % 2
    home = core == y_lo
    spot = jnp.stack([x_id, core, lax.axis_index("col"), home.astype(jnp.int32)]).astype(jnp.int32)
    run = Chain()

    swap = lambda value: lax.ppermute(value, "row", core_swap)
    cross = lambda value: lax.ppermute(value, "row", half_swap)
    right = lambda value: lax.ppermute(value, "depth", x_shift(1))
    left = lambda value: lax.ppermute(value, "depth", x_shift(-1))
    home_one = lambda value: lax.ppermute(value, ("depth", "row"), home_first)
    home_two = lambda value: lax.ppermute(value, ("depth", "row"), home_second)
    trade = lambda value: lax.all_to_all(value, "col", 0, 0, tiled=True)

    half = gate_weight.shape[1] // 2
    far, near, last = (2,), (1, 3), (0,)
    oth_columns = lambda value: lax.dynamic_slice_in_dim(value, (1 - core) * half, half, 1)
    oth_rows = lambda value: lax.dynamic_slice_in_dim(value, (1 - core) * half, half, 0)

    tokens_oth = swap(tokens)
    output_grad_oth = swap(output_grad)
    grad_halves = [output_grad, output_grad_oth]
    gate_oth = swap(run(oth_columns, gate_weight))
    up_oth = swap(run(oth_columns, after(up_weight, tokens_oth)))
    gate_up_of = lambda steps: run(
        functools.partial(gate_up_partial, steps),
        spot, tokens, tokens_oth, gate_weight, up_weight, gate_oth, up_oth,
    )
    part_far, send = gate_up_of(far)
    got_far = cross(send)
    down_oth = swap(run(oth_rows, down_weight))
    part_near, send = gate_up_of(near)
    got_near = cross(after(send, got_far))

    hidden_far, hidden_t = run(hidden_step, part_far, got_far)
    down_far = run(lambda a, b0, b1: far_terms(1, (a, a), (b0, b1)), hidden_t, *grad_halves)
    down_far = (right(down_far[0]), left(down_far[1]))
    joint = lambda gate_up_step, hg_steps: run(
        functools.partial(joint_partial, gate_up_step, hg_steps),
        spot,
        (tokens, tokens_oth),
        (gate_weight, up_weight, gate_oth, up_oth),
        grad_halves,
        (down_weight, down_oth),
    )
    part_last, hg_far, send = joint(last[0], far)
    got_last = cross(after(send, got_near))

    hidden_near, hidden_t = run(hidden_step, part_near, got_near)
    t_spec = [window((wide, rows), (0, 0))] * 2 + [window((wide, rows), (1, 0))] * 2
    o_spec = [window((rows, feat), (0, 0))] * 4
    f_spec = [window((wide, feat), (0, 0))] * 2
    down_near = run(
        lambda a, b0, b1, r, l: near_terms(
            (a, a, a, a, b0, b1, b0, b1, r, l), t_spec + o_spec + f_spec, wide, feat
        ),
        hidden_t, *grad_halves, *down_far,
    )
    down_near = (right(down_near[0]), left(down_near[1]))
    hg_rest, send = joint(None, near + last)
    hg_got = cross(after(send, got_last))
    tokens_t = [run(jnp.transpose, value) for value in (tokens, tokens_oth)]

    grads_far = run(functools.partial(grads_step, 0, 2), part_far, got_far, hg_far, got_last)
    gate_up_far = run(lambda b, a0, a1: far_terms(1, (a0, a1), (b, b)), grads_far, *tokens_t)
    gate_up_far = (right(gate_up_far[0]), left(gate_up_far[1]))
    hidden_last, hidden_t = run(hidden_step, part_last, got_last)
    down_spec = (
        [((wide, rows), (0, 0))] * 2 + [((rows, feat), (0, 0))] * 2 + [((2 * wide, feat), (0, 0))] * 2
    )
    down_keep, first, second = run(
        lambda s, a, b0, b1, l, r: last_terms(s, (a, a, b0, b1, l, r), down_spec, wide, feat),
        spot, hidden_t, *grad_halves, *down_near,
    )
    down_first, down_second = home_one(first), home_two(second)
    hidden = (hidden_far, hidden_near, hidden_last)
    mlp_of = lambda block_of, dtype, weight: run(
        lambda s, w, *v: activation_part(mlp_body, block_of, dtype, "mlp_part", s, v, [w], True),
        spot, weight, *hidden,
    )
    mlp_oth = swap(mlp_of(oth_block, bf16, down_oth))
    mlp_own = mlp_of(own_block, f32, down_weight)
    grads_near = run(functools.partial(grads_step, 0, 0), part_near, got_near, hg_rest, hg_got)
    grads_last = run(functools.partial(grads_step, 2, 2), part_last, got_last, hg_rest, hg_got)
    grads = (grads_far, grads_near, grads_last)
    two = 2 * wide
    specs = [window((feat, rows), (0, 0))] * 4
    specs += [window((rows, two), (0, 0))] * 2 + [window((rows, two), (0, 1))] * 2
    specs += [window((feat, two), (0, 0))] * 2
    gate_up_near = run(
        lambda b, a0, a1, *got: near_terms((a0, a1, a0, a1, b, b, b, b, *got), specs, feat, two),
        grads_near, *tokens_t, *gate_up_far,
    )
    gate_up_near = (right(gate_up_near[0]), left(gate_up_near[1]))
    mlp_sum = lax.psum_scatter(
        run(functools.partial(join, f32), mlp_own, mlp_oth), "col", scatter_dimension=0, tiled=True
    )
    input_of = lambda block_of, dtype, *weights: run(
        lambda s, g, u, *v: activation_part(input_body, block_of, dtype, "input_part", s, v, [g, u], False),
        spot, *weights, *grads,
    )
    input_oth = swap(input_of(oth_block, bf16, gate_oth, up_oth))
    input_own = input_of(own_block, f32, gate_weight, up_weight)
    input_parts = trade(run(functools.partial(join, bf16), input_own, input_oth))

    (down_out,) = run(functools.partial(finish, 1), spot, down_first, down_keep, down_second)
    end_spec = [((feat, rows), (0, 0))] * 2 + [((rows, two), (0, 0))] * 2 + [((2 * feat, two), (0, 0))] * 2
    gate_up_keep, first, second = run(
        lambda s, a0, a1, b, l, r: last_terms(s, (a0, a1, b, b, l, r), end_spec, feat, two),
        spot, *tokens_t, grads_last, *gate_up_near,
    )
    gate_up_first, gate_up_second = home_one(first), home_two(second)
    both = lax.all_gather(run(collect, mlp_sum, input_parts), "col", axis=0, tiled=True)
    mlp_output, input_grad = both[:, :feat], both[:, feat:]
    gate_out, up_out = run(functools.partial(finish, 2), spot, gate_up_first, gate_up_keep, gate_up_second)
    return (mlp_output, input_grad, gate_out, up_out, down_out)


def solution(mesh):
    placed = (
        P("depth", "row"),
        P("row", "col"),
        P("row", "col"),
        P("col", "row"),
        P("depth", "row"),
    )
    return jax.shard_map(
        local,
        mesh=mesh,
        in_specs=placed,
        out_specs=(
            P("depth", "row"),
            P("depth", "row"),
            P("depth", "row", "col"),
            P("depth", "row", "col"),
            P("depth", "col", "row"),
        ),
        check_vma=False,
    )
```

time: 478 us -> 221 us (0.46)
  waiting for transfers between devices: 334 us -> 73 us
  blocking collectives: 67.2 us -> 0 us
  Pallas kernels: 0 us -> 57 us
  starting transfers between devices: 0.47 us -> 44.3 us
  matrix products: 39.2 us -> 0 us
  local copies, waits for them, and re-layouts: 6.48 us -> 27.4 us
  other arithmetic: 15.9 us -> 0.67 us
    reduce_scatter x5 -> x1, waiting for transfers between devices: 271 us -> 0.01 us  [local(): lax.psum_scatter(run(functools.partial(join, f32), mlp_own, mlp_oth), 'co...]
    psum x1 -> x0, blocking collectives: 67.2 us -> none  [local(): mlp_output = lax.psum(partial_value, 'col').astype(jnp.bfloat16)]
    ppermute x0 -> x23, waiting for transfers between devices: none -> 61 us  [the longest x4 24.6 us: local(): cross = lambda value: lax.ppermute(value, 'row', half_swap)]
    pallas_call x0 -> x25, Pallas kernels: none -> 57 us  [the longest x4 13.2 us: activation_part(): pl.pallas_call(body, grid_spec=pltpu.PrefetchScalarGridSpec(num_scalar_pr...]
    all_gather x2 -> x1, waiting for transfers between devices: 62.7 us -> 12 us  [local(): lax.all_gather(run(collect, mlp_sum, input_parts), 'col', axis=0, tiled=T...]
    dot_general x9 -> x0, matrix products: 39.2 us -> none  [the longest x6 28.4 us: contract(): lax.dot_general(left_array, right_array, (((left_axis,), (right_axis,)),...]
    ppermute x0 -> x23, starting transfers between devices: none -> 36.2 us  [the longest x7 11.4 us: local(): swap = lambda value: lax.ppermute(value, 'row', core_swap)]
    unnamed x14 -> x95, local copies, waits for them, and re-layouts: 6.48 us -> 19 us
  transfers between devices with their start and end apart: 7 -> 26, of which waited for: 6 -> 13; matrix products, arithmetic and copies ran while one was open for 10% -> 3% of each run, Pallas kernels for 0% -> 24%
where the time goes in v1:
time: 221 us; the launch traced here: 217 us
  waiting for transfers between devices  73 us (33%)
  Pallas kernels  57 us (26%)
  starting transfers between devices  44.3 us (20%)
  local copies, waits for them, and re-layouts  27.4 us (12%)
  between operations  14.5 us (7%)
    ppermute x4, waiting for transfers between devices, local(): cross = lambda value: lax.ppermute(value, 'row', half_swap)  24.6 us
    ppermute x2, waiting for transfers between devices, local(): home_two = lambda value: lax.ppermute(value, ('depth', 'row'), home_second)  19.6 us
    unnamed x95, local copies, waits for them, and re-layouts  19 us
    pallas_call x4, Pallas kernels, activation_part(): pl.pallas_call(body, grid_spec=pltpu.PrefetchScalarGridSpec(num_scalar_pr...  13.2 us
    all_gather x1, waiting for transfers between devices, local(): lax.all_gather(run(collect, mlp_sum, input_parts), 'col', axis=0, tiled=T...  12 us
    pallas_call x2, Pallas kernels, joint_partial(): pl.pallas_call(functools.partial(joint_body, gate_up_step, hg_steps), gri...  11.8 us
    pallas_call x2, Pallas kernels, gate_up_partial(): pl.pallas_call(gate_up_body, grid_spec=pltpu.PrefetchScalarGridSpec(num_s...  11.6 us
    ppermute x7, starting transfers between devices, local(): swap = lambda value: lax.ppermute(value, 'row', core_swap)  11.4 us
  transfers between devices with their start and end apart: 26, of which 13 were waited for; matrix products, arithmetic and copies ran while one was open for 3% of the time, Pallas kernels for 24%

profile of v1, /device:TPU:1, one launch (start us, length us, event | category | flops | bytes accessed | tf_op | source)
XLA Modules:
  0.0 216.9 jit_solution(2429957256344027967)
XLA Ops:
  8.6 3.3 %collective-permute-start = (bf16[512,768]{0,1:T(8,128)(2,1)S(1)}, bf16[512,768]{0,1:T(8,128)(2,1)S(1)}, u32[]{:S(2)}, u32[]{:S(2)}) collective-permute-start(bf16[512,768]{0,1:T(8,128)(2,1)S(1)} %copy.10), channel_id=1, source_target_pairs={{0,8},{8,0},{16,24},{24,16},{1,9},{9,1},{17,25},{25,17},{2,10},{10... | collective-permute-start | bytes 2359304 | tf_op jit(solution)/shard_map/ppermute | solution.py:456
  17.6 2.2 collective-permute-done.2.oth_up_ref.refs_5_.u2.u1.u3.u0
  19.7 4.4 %gate_up_partial.2 = (f32[512,512]{1,0:T(8,128)}, bf16[512,512]{1,0:T(8,128)(2,1)}) custom-call(s32[4]{0:T(128)} %pad_add_fusion.spot, bf16[512,768]{1,0:T(8,128)(2,1)} %refs_0_.2, bf16[512,768]{1,0:T(8,128)(2,1)} %copy.11.oth_ref.refs_1_, bf16[768,2048]{1,0:T(8,128)(2,1)} %g0.1, bf16[768,2048]{1,0:T(8,128)(2,1)} %u0.1, ...), custom_call_target="tpu_custom_call" | custom-call | flops 1 | bytes 14850000 | tf_op jit(solution)/shard_map/gate_up_partial/pallas_call | solution.py:98
  27.1 7.2 %gate_up_partial.3 = (f32[512,1024]{1,0:T(8,128)}, bf16[512,1024]{1,0:T(8,128)(2,1)}) custom-call(s32[4]{0:T(128)} %pad_add_fusion.spot, bf16[512,768]{1,0:T(8,128)(2,1)} %refs_0_.2, bf16[512,768]{1,0:T(8,128)(2,1)} %copy.11.oth_ref.refs_1_, bf16[768,2048]{1,0:T(8,128)(2,1)} %g0.1, bf16[768,2048]{1,0:T(8,128)(2,1)} %u0.1, ...), custom_call_target="tpu_custom_call" | custom-call | flops 1 | bytes 14850000 | tf_op jit(solution)/shard_map/gate_up_partial/pallas_call | solution.py:98
  34.4 4.9 %collective-permute-done.3.got_ref = bf16[512,512]{1,0:T(8,128)(2,1)S(1)} collective-permute-done((bf16[512,512]{1,0:T(8,128)(2,1)}, bf16[512,512]{1,0:T(8,128)(2,1)S(1)}, u32[]{:S(2)}, u32[]{:S(2)}) %collective-permute-start.3) | collective-permute-done | bytes 524320 | tf_op jit(solution)/shard_map/ppermute | solution.py:457
  42.0 2.6 %collective-permute-start.8 = (bf16[256,768]{1,0:T(8,128)(2,1)S(1)}, bf16[256,768]{1,0:T(8,128)(2,1)S(1)}, u32[]{:S(2)}, u32[]{:S(2)}) collective-permute-start(bf16[256,768]{1,0:T(8,128)(2,1)S(1)} %get-tuple-element.89), channel_id=1, source_target_pairs={{0,96},{32,0},{64,32},{96,64},{128,224},{160,128},{192,160},{224,1... | collective-permute-start | bytes 1179656 | tf_op jit(solution)/shard_map/ppermute | solution.py:459
  45.7 6.2 %joint_partial.2 = (f32[512,512]{1,0:T(8,128)}, f32[512,256]{1,0:T(8,128)}, bf16[512,768]{1,0:T(8,128)(2,1)}) custom-call(s32[4]{0:T(128)} %pad_add_fusion.spot, bf16[512,768]{1,0:T(8,128)(2,1)} %refs_0_.2, bf16[512,768]{1,0:T(8,128)(2,1)} %copy.11.oth_ref.refs_1_, bf16[768,2048]{1,0:T(8,128)(2,1)} %g0.1, bf16[768,2048]{1,0:T(8,128)(2,1)} %u0.1, ...), custom_call_target="tpu_custom_call" | custom-call | flops 1 | bytes 19800000 | tf_op jit(solution)/shard_map/joint_partial/pallas_call | solution.py:156
  51.9 12.8 %collective-permute-done.6.got_ref = bf16[512,1024]{1,0:T(8,128)(2,1)S(1)} collective-permute-done((bf16[512,1024]{1,0:T(8,128)(2,1)}, bf16[512,1024]{1,0:T(8,128)(2,1)S(1)}, u32[]{:S(2)}, u32[]{:S(2)}) %collective-permute-start.6) | collective-permute-done | bytes 1048608 | tf_op jit(solution)/shard_map/ppermute | solution.py:457
  69.4 2.5 %collective-permute-start.11 = (bf16[512,768]{1,0:T(8,128)(2,1)}, bf16[512,768]{1,0:T(8,128)(2,1)}, u32[]{:S(2)}, u32[]{:S(2)}) collective-permute-start(bf16[512,768]{1,0:T(8,128)(2,1)} %get-tuple-element.105), channel_id=1, source_target_pairs={{0,96},{32,0},{64,32},{96,64},{128,224},{160,128},{192,160},{224,1... | collective-permute-start | bytes 2359304 | tf_op jit(solution)/shard_map/ppermute | solution.py:459
  71.9 5.7 %joint_partial.3 = (f32[512,768]{1,0:T(8,128)}, bf16[512,768]{1,0:T(8,128)(2,1)}) custom-call(s32[4]{0:T(128)} %pad_add_fusion.spot, bf16[512,768]{1,0:T(8,128)(2,1)} %b0.5, bf16[512,768]{1,0:T(8,128)(2,1)} %copy-done.10, bf16[2048,768]{1,0:T(8,128)(2,1)} %w0.1, bf16[1024,768]{1,0:T(8,128)(2,1)} %copy-done.5, bf16[2048,768]{1,0:T(8,128)(2,1)} %w0.1, ...), custom_call_target="tpu_custom_call" | custom-call | flops 1 | bytes 19800000 | tf_op jit(solution)/shard_map/joint_partial/pallas_call | solution.py:156
  77.9 5.7 %collective-permute-done.9.hg_got_ref.got_ref = bf16[512,768]{1,0:T(8,128)(2,1)S(1)} collective-permute-done((bf16[512,768]{1,0:T(8,128)(2,1)}, bf16[512,768]{1,0:T(8,128)(2,1)S(1)}, u32[]{:S(2)}, u32[]{:S(2)}) %collective-permute-start.9) | collective-permute-done | bytes 786464 | tf_op jit(solution)/shard_map/ppermute | solution.py:457
  88.4 2.1 collective-permute-start.12
  92.6 2.7 %last_terms.2 = (f32[256,768]{1,0:T(8,128)S(1)}, bf16[256,768]{1,0:T(8,128)(2,1)S(1)}, bf16[256,768]{1,0:T(8,128)(2,1)S(1)}) custom-call(s32[4]{0:T(128)S(1)} %copy-done.41, bf16[256,512]{1,0:T(8,128)(2,1)S(1)} %get-tuple-element.104.a0.a1, bf16[256,512]{1,0:T(8,128)(2,1)S(1)} %get-tuple-element.104.a0.a1, bf16[512,768]{1,0:T(8,128)(2,1)S(1)} %copy-done.9, ...), custom_call_target="tpu_custom_call" | custom-call | flops 1 | bytes 4290000 | tf_op jit(solution)/shard_map/last_terms/pallas_call | solution.py:371
  96.9 2.2 %mlp_part.2 = bf16[512,768]{1,0:T(8,128)(2,1)S(1)} custom-call(s32[4]{0:T(128)S(1)} %copy-done.41, bf16[512,256]{1,0:T(8,128)(2,1)S(1)} %copy-done.36, bf16[512,512]{1,0:T(8,128)(2,1)S(1)} %copy-done.30, bf16[512,256]{1,0:T(8,128)(2,1)S(1)} %get-tuple-element.102.last_ref, bf16[1024,768]{1,0:T(8,128)(2,1)S(1)} %copy-done.6, bf16[1024,768]{1,0:T(8,128)(2,1)S(1)} %copy-done.6, ...), custom_call_target="tpu_custom_call" | custom-call | flops 1 | bytes 8250000 | tf_op jit(solution)/shard_map/mlp_part/pallas_call | solution.py:262
  99.2 3.6 %collective-permute-start.15 = (bf16[512,768]{1,0:T(8,128)(2,1)S(1)}, bf16[512,768]{1,0:T(8,128)(2,1)S(1)}, u32[]{:S(2)}, u32[]{:S(2)}) collective-permute-start(bf16[512,768]{1,0:T(8,128)(2,1)S(1)} %mlp_part.2), channel_id=1, source_target_pairs={{0,8},{8,0},{16,24},{24,16},{1,9},{9,1},{17,25},{25,17},{2,10},{10... | collective-permute-start | bytes 2359304 | tf_op jit(solution)/shard_map/ppermute | solution.py:456
  102.7 2.3 %mlp_part.3.own_ref = f32[512,768]{1,0:T(8,128)S(1)} custom-call(s32[4]{0:T(128)S(1)} %copy-done.41, bf16[512,256]{1,0:T(8,128)(2,1)S(1)} %copy-done.36, bf16[512,512]{1,0:T(8,128)(2,1)S(1)} %copy-done.30, bf16[512,256]{1,0:T(8,128)(2,1)S(1)} %get-tuple-element.102.last_ref, bf16[2048,768]{1,0:T(8,128)(2,1)S(1)} %copy-done.1, ...), custom_call_target="tpu_custom_call" | custom-call | flops 1 | bytes 8250000 | tf_op jit(solution)/shard_map/mlp_part/pallas_call | solution.py:262
  107.6 3.1 %near_terms.3 = (bf16[1536,512]{1,0:T(8,128)(2,1)}, bf16[1536,512]{1,0:T(8,128)(2,1)}) custom-call(bf16[768,512]{1,0:T(8,128)(2,1)S(1)} %bitcast.13, bf16[768,512]{1,0:T(8,128)(2,1)S(1)} %bitcast.9, bf16[768,512]{1,0:T(8,128)(2,1)S(1)} %bitcast.14, bf16[768,512]{1,0:T(8,128)(2,1)S(1)} %bitcast.10, bf16[512,1024]{1,0:T(8,128)(2,1)S(1)} %grads_step.4.b0.b1.d0.d1.near_ref, ...), custom_call_target="tpu_custom_call" | custom-call | flops 1 | bytes 7260000 | tf_op jit(solution)/shard_map/near_terms/pallas_call | solution.py:340
  113.1 5.1 %input_part.2 = bf16[512,768]{1,0:T(8,128)(2,1)S(1)} custom-call(s32[4]{0:T(128)S(1)} %copy-done.41, bf16[512,512]{1,0:T(8,128)(2,1)S(1)} %copy-done.16, bf16[512,1024]{1,0:T(8,128)(2,1)S(1)} %grads_step.4.b0.b1.d0.d1.near_ref, bf16[512,512]{1,0:T(8,128)(2,1)S(1)} %grads_step.5.last_ref.b0.b1, ...), custom_call_target="tpu_custom_call" | custom-call | flops 1 | bytes 8250000 | tf_op jit(solution)/shard_map/input_part/pallas_call | solution.py:262
  118.2 3.8 %collective-permute-start.16 = (bf16[512,768]{1,0:T(8,128)(2,1)S(1)}, bf16[512,768]{1,0:T(8,128)(2,1)S(1)}, u32[]{:S(2)}, u32[]{:S(2)}) collective-permute-start(bf16[512,768]{1,0:T(8,128)(2,1)S(1)} %input_part.2), channel_id=1, source_target_pairs={{0,8},{8,0},{16,24},{24,16},{1,9},{9,1},{17,25},{25,17},{2,10},{10... | collective-permute-start | bytes 2359304 | tf_op jit(solution)/shard_map/ppermute | solution.py:456
  122.0 2.5 %collective-permute-start.20 = (bf16[1536,512]{1,0:T(8,128)(2,1)}, bf16[1536,512]{1,0:T(8,128)(2,1)}, u32[]{:S(2)}, u32[]{:S(2)}) collective-permute-start(bf16[1536,512]{1,0:T(8,128)(2,1)} %get-tuple-element.123), channel_id=1, source_target_pairs={{0,96},{32,0},{64,32},{96,64},{128,224},{160,128},{192,160},{224,1... | collective-permute-start | bytes 4718600 | tf_op jit(solution)/shard_map/ppermute | solution.py:459
  124.5 3.6 %input_part.3.own_ref = f32[512,768]{1,0:T(8,128)S(1)} custom-call(s32[4]{0:T(128)S(1)} %copy-done.41, bf16[512,512]{1,0:T(8,128)(2,1)S(1)} %copy-done.16, bf16[512,1024]{1,0:T(8,128)(2,1)S(1)} %grads_step.4.b0.b1.d0.d1.near_ref, bf16[512,512]{1,0:T(8,128)(2,1)S(1)} %grads_step.5.last_ref.b0.b1, bf16[768,2048]{1,0:T(8,128)(2,1)S(1)} %copy-done.2, ...), custom_call_target="tpu_custom_call" | custom-call | flops 1 | bytes 8250000 | tf_op jit(solution)/shard_map/input_part/pallas_call | solution.py:262
  129.2 8.1 %all-to-all-start = ((bf16[8,64,768]{2,1,0:T(8,128)(2,1)}), bf16[8,64,768]{2,1,0:T(8,128)(2,1)S(1)}, u32[]{:S(2)}, u32[]{:S(2)}) async-start(bf16[8,64,768]{2,1,0:T(8,128)(2,1)} %bitcast.17), calls=%async_computation.1 | async-start | bytes 1572864 | tf_op jit(solution)/shard_map/all_to_all | solution.py:462
  137.7 3.9 %collective-permute-start.18 = (bf16[256,768]{1,0:T(8,128)(2,1)S(1)}, bf16[256,768]{1,0:T(8,128)(2,1)S(1)}, u32[]{:S(2)}, u32[]{:S(2)}) collective-permute-start(bf16[256,768]{1,0:T(8,128)(2,1)S(1)} %get-tuple-element.121), channel_id=1, source_target_pairs={{8,128},{24,144},{40,160},{56,176},{72,192},{88,208},{104,224},{12... | collective-permute-start | bytes 1179656 | tf_op jit(solution)/shard_map/ppermute | solution.py:461
  142.7 7.2 %collective-permute-done.18.two_ref = bf16[256,768]{1,0:T(8,128)(2,1)S(1)} collective-permute-done((bf16[256,768]{1,0:T(8,128)(2,1)S(1)}, bf16[256,768]{1,0:T(8,128)(2,1)S(1)}, u32[]{:S(2)}, u32[]{:S(2)}) %collective-permute-start.18) | collective-permute-done | bytes 393248 | tf_op jit(solution)/shard_map/ppermute | solution.py:461
  152.6 5.9 %collective-permute-done.20.from_right = bf16[1536,512]{1,0:T(8,128)(2,1)} collective-permute-done((bf16[1536,512]{1,0:T(8,128)(2,1)}, bf16[1536,512]{1,0:T(8,128)(2,1)}, u32[]{:S(2)}, u32[]{:S(2)}) %collective-permute-start.20) | collective-permute-done | bytes 1572896 | tf_op jit(solution)/shard_map/ppermute | solution.py:459
  158.5 3.1 %collective-permute-done.19.from_left = bf16[1536,512]{1,0:T(8,128)(2,1)} collective-permute-done((bf16[1536,512]{1,0:T(8,128)(2,1)}, bf16[1536,512]{1,0:T(8,128)(2,1)}, u32[]{:S(2)}, u32[]{:S(2)}) %collective-permute-start.19) | collective-permute-done | bytes 1572896 | tf_op jit(solution)/shard_map/ppermute | solution.py:458
  161.6 3.6 %last_terms.3 = (f32[768,512]{1,0:T(8,128)S(1)}, bf16[768,512]{1,0:T(8,128)(2,1)S(1)}, bf16[768,512]{1,0:T(8,128)(2,1)S(1)}) custom-call(s32[4]{0:T(128)S(1)} %copy-done.41, bf16[768,512]{1,0:T(8,128)(2,1)S(1)} %bitcast.15, bf16[768,512]{1,0:T(8,128)(2,1)S(1)} %bitcast.11, bf16[512,512]{1,0:T(8,128)(2,1)S(1)} %grads_step.5.last_ref.b0.b1, ...), custom_call_target="tpu_custom_call" | custom-call | flops 1 | bytes 4290000 | tf_op jit(solution)/shard_map/last_terms/pallas_call | solution.py:371
  170.6 4.8 %collective-permute-start.22 = (bf16[768,512]{1,0:T(8,128)(2,1)}, bf16[768,512]{1,0:T(8,128)(2,1)S(1)}, u32[]{:S(2)}, u32[]{:S(2)}) collective-permute-start(bf16[768,512]{1,0:T(8,128)(2,1)} %copy-done.42), channel_id=1, source_target_pairs={{8,128},{24,144},{40,160},{56,176},{72,192},{88,208},{104,224},{12... | collective-permute-start | bytes 2359304 | tf_op jit(solution)/shard_map/ppermute | solution.py:461
  175.4 4.4 %collective-permute-done.21.one_ref = bf16[768,512]{1,0:T(8,128)(2,1)S(1)} collective-permute-done((bf16[768,512]{1,0:T(8,128)(2,1)}, bf16[768,512]{1,0:T(8,128)(2,1)S(1)}, u32[]{:S(2)}, u32[]{:S(2)}) %collective-permute-start.21) | collective-permute-done | bytes 786464 | tf_op jit(solution)/shard_map/ppermute | solution.py:460
  179.8 12.4 %collective-permute-done.22.two_ref = bf16[768,512]{1,0:T(8,128)(2,1)S(1)} collective-permute-done((bf16[768,512]{1,0:T(8,128)(2,1)}, bf16[768,512]{1,0:T(8,128)(2,1)S(1)}, u32[]{:S(2)}, u32[]{:S(2)}) %collective-permute-start.22) | collective-permute-done | bytes 786464 | tf_op jit(solution)/shard_map/ppermute | solution.py:461
  195.5 12.0 %all-gather.2.cloned.1.call-done = bf16[512,1536]{1,0:T(8,128)(2,1)} async-done(((bf16[64,1536]{1,0:T(8,128)(2,1)}), bf16[512,1536]{1,0:T(8,128)(2,1)}) %all-gather.2.cloned.1.call-update) | async-done | bytes 1572880 | tf_op jit(solution)/shard_map/all_gather | solution.py:562
  207.5 2.6 %fusion = (bf16[512,768]{1,0:T(8,128)(2,1)}, bf16[512,768]{1,0:T(8,128)(2,1)}) fusion(bf16[512,1536]{1,0:T(8,128)(2,1)} %all-gather.2.cloned.1.call-done), kind=kLoop, calls=%fused_computation.4 | loop fusion | bytes 3145728 | tf_op jit(solution)/shard_map/slice | solution.py:563
  (149 shorter events, 46.2 us)
Async XLA Ops:
  7.2 160.9 %reduce-scatter.2.cloned.1.call-start = ((), (), s32[]{:S(2)}) async-start(), calls=%async_computation.2 | async-start | bytes 1769472 | tf_op jit(solution)/shard_map/reduce_scatter | solution.py:544
  8.6 5.2 %collective-permute-start = (bf16[512,768]{0,1:T(8,128)(2,1)S(1)}, bf16[512,768]{0,1:T(8,128)(2,1)S(1)}, u32[]{:S(2)}, u32[]{:S(2)}) collective-permute-start(bf16[512,768]{0,1:T(8,128)(2,1)S(1)} %copy.10), channel_id=1, source_target_pairs={{0,8},{8,0},{16,24},{24,16},{1,9},{9,1},{17,25},{25,17},{2,10},{10... | collective-permute-start | bytes 2359304 | tf_op jit(solution)/shard_map/ppermute | solution.py:456
  13.6 3.9 %collective-permute-start.1 = (bf16[768,1024]{1,0:T(8,128)(2,1)S(1)}, bf16[768,1024]{1,0:T(8,128)(2,1)}, u32[]{:S(2)}, u32[]{:S(2)}) collective-permute-start(bf16[768,1024]{1,0:T(8,128)(2,1)S(1)} %constant_dynamic-slice_fusion.2), channel_id=1, source_target_pairs={{0,8},{8,0},{16,24},{24,16},{1,9},{9,1},{17,25},{25,17},{2,10},{10... | collective-permute-start | bytes 4718600 | tf_op jit(solution)/shard_map/ppermute | solution.py:456
  15.7 4.0 %collective-permute-start.2 = (bf16[768,1024]{1,0:T(8,128)(2,1)}, bf16[768,1024]{1,0:T(8,128)(2,1)}, u32[]{:S(2)}, u32[]{:S(2)}) collective-permute-start(bf16[768,1024]{1,0:T(8,128)(2,1)} %constant_dynamic-slice_fusion.1), channel_id=1, source_target_pairs={{0,8},{8,0},{16,24},{24,16},{1,9},{9,1},{17,25},{25,17},{2,10},{10... | collective-permute-start | bytes 4718600 | tf_op jit(solution)/shard_map/ppermute | solution.py:456
  17.6 7.8 %copy-start = (bf16[2048,768]{1,0:T(8,128)(2,1)S(1)}, bf16[2048,768]{1,0:T(8,128)(2,1)}, u32[]{:S(2)}) copy-start(bf16[2048,768]{1,0:T(8,128)(2,1)} %w0.1) | copy-start | bytes 9437188
  24.1 15.2 %collective-permute-start.3 = (bf16[512,512]{1,0:T(8,128)(2,1)}, bf16[512,512]{1,0:T(8,128)(2,1)S(1)}, u32[]{:S(2)}, u32[]{:S(2)}) collective-permute-start(bf16[512,512]{1,0:T(8,128)(2,1)} %get-tuple-element.76), channel_id=1, source_target_pairs={{0,16},{16,0},{8,24},{24,8},{1,17},{17,1},{9,25},{25,9},{2,18},{18... | collective-permute-start | bytes 1572872 | tf_op jit(solution)/shard_map/ppermute | solution.py:457
  26.6 13.8 %copy-start.25 = (f32[512,512]{1,0:T(8,128)S(1)}, f32[512,512]{1,0:T(8,128)}, u32[]{:S(2)}) copy-start(f32[512,512]{1,0:T(8,128)} %get-tuple-element.95.part_ref) | copy-start | bytes 3145732
  26.6 17.9 %collective-permute-start.5 = (bf16[1024,768]{1,0:T(8,128)(2,1)}, bf16[1024,768]{1,0:T(8,128)(2,1)S(1)}, u32[]{:S(2)}, u32[]{:S(2)}) collective-permute-start(bf16[1024,768]{1,0:T(8,128)(2,1)} %constant_dynamic-slice_fusion), channel_id=1, source_target_pairs={{0,8},{8,0},{16,24},{24,16},{1,9},{9,1},{17,25},{25,17},{2,10},{10... | collective-permute-start | bytes 4718600 | tf_op jit(solution)/shard_map/ppermute | solution.py:456
  27.0 14.3 %collective-permute-start.4 = (bf16[512,768]{1,0:T(8,128)(2,1)S(1)}, bf16[512,768]{1,0:T(8,128)(2,1)S(1)}, u32[]{:S(2)}, u32[]{:S(2)}) collective-permute-start(bf16[512,768]{1,0:T(8,128)(2,1)S(1)} %copy-done.7), channel_id=1, source_target_pairs={{0,8},{8,0},{16,24},{24,16},{1,9},{9,1},{17,25},{25,17},{2,10},{10... | collective-permute-start | bytes 2359304 | tf_op jit(solution)/shard_map/ppermute | solution.py:456
  39.3 25.4 %collective-permute-start.6 = (bf16[512,1024]{1,0:T(8,128)(2,1)}, bf16[512,1024]{1,0:T(8,128)(2,1)S(1)}, u32[]{:S(2)}, u32[]{:S(2)}) collective-permute-start(bf16[512,1024]{1,0:T(8,128)(2,1)} %get-tuple-element.85), channel_id=1, source_target_pairs={{0,16},{16,0},{8,24},{24,8},{1,17},{17,1},{9,25},{25,9},{2,18},{18... | collective-permute-start | bytes 3145736 | tf_op jit(solution)/shard_map/ppermute | solution.py:457
  42.0 25.4 %collective-permute-start.8 = (bf16[256,768]{1,0:T(8,128)(2,1)S(1)}, bf16[256,768]{1,0:T(8,128)(2,1)S(1)}, u32[]{:S(2)}, u32[]{:S(2)}) collective-permute-start(bf16[256,768]{1,0:T(8,128)(2,1)S(1)} %get-tuple-element.89), channel_id=1, source_target_pairs={{0,96},{32,0},{64,32},{96,64},{128,224},{160,128},{192,160},{224,1... | collective-permute-start | bytes 1179656 | tf_op jit(solution)/shard_map/ppermute | solution.py:459
  44.5 21.3 %copy-start.17 = (f32[512,1024]{1,0:T(8,128)S(1)}, f32[512,1024]{1,0:T(8,128)}, u32[]{:S(2)}) copy-start(f32[512,1024]{1,0:T(8,128)} %get-tuple-element.109.part_ref) | copy-start | bytes 6291460
  44.5 22.9 %collective-permute-start.7 = (bf16[256,768]{1,0:T(8,128)(2,1)S(1)}, bf16[256,768]{1,0:T(8,128)(2,1)S(1)}, u32[]{:S(2)}, u32[]{:S(2)}) collective-permute-start(bf16[256,768]{1,0:T(8,128)(2,1)S(1)} %get-tuple-element.80), channel_id=1, source_target_pairs={{0,32},{32,64},{64,96},{96,0},{128,160},{160,192},{192,224},{224,1... | collective-permute-start | bytes 1179656 | tf_op jit(solution)/shard_map/ppermute | solution.py:458
  64.7 18.9 %collective-permute-start.9 = (bf16[512,768]{1,0:T(8,128)(2,1)}, bf16[512,768]{1,0:T(8,128)(2,1)S(1)}, u32[]{:S(2)}, u32[]{:S(2)}) collective-permute-start(bf16[512,768]{1,0:T(8,128)(2,1)} %get-tuple-element.98), channel_id=1, source_target_pairs={{0,16},{16,0},{8,24},{24,8},{1,17},{17,1},{9,25},{25,9},{2,18},{18... | collective-permute-start | bytes 2359304 | tf_op jit(solution)/shard_map/ppermute | solution.py:457
  69.4 23.1 %collective-permute-start.11 = (bf16[512,768]{1,0:T(8,128)(2,1)}, bf16[512,768]{1,0:T(8,128)(2,1)}, u32[]{:S(2)}, u32[]{:S(2)}) collective-permute-start(bf16[512,768]{1,0:T(8,128)(2,1)} %get-tuple-element.105), channel_id=1, source_target_pairs={{0,96},{32,0},{64,32},{96,64},{128,224},{160,128},{192,160},{224,1... | collective-permute-start | bytes 2359304 | tf_op jit(solution)/shard_map/ppermute | solution.py:459
  71.9 20.6 %collective-permute-start.10 = (bf16[512,768]{1,0:T(8,128)(2,1)}, bf16[512,768]{1,0:T(8,128)(2,1)}, u32[]{:S(2)}, u32[]{:S(2)}) collective-permute-start(bf16[512,768]{1,0:T(8,128)(2,1)} %get-tuple-element.90), channel_id=1, source_target_pairs={{0,32},{32,64},{64,96},{96,0},{128,160},{160,192},{192,224},{224,1... | collective-permute-start | bytes 2359304 | tf_op jit(solution)/shard_map/ppermute | solution.py:458
  88.1 19.5 %collective-permute-start.13 = (bf16[768,512]{1,0:T(8,128)(2,1)S(1)}, bf16[768,512]{1,0:T(8,128)(2,1)S(1)}, u32[]{:S(2)}, u32[]{:S(2)}) collective-permute-start(bf16[768,512]{1,0:T(8,128)(2,1)S(1)} %get-tuple-element.100), channel_id=1, source_target_pairs={{0,32},{32,64},{64,96},{96,0},{128,160},{160,192},{192,224},{224,1... | collective-permute-start | bytes 2359304 | tf_op jit(solution)/shard_map/ppermute | solution.py:458
  88.4 17.8 %collective-permute-start.12 = (bf16[512,768]{1,0:T(8,128)(2,1)S(1)}, bf16[512,768]{1,0:T(8,128)(2,1)S(1)}, u32[]{:S(2)}, u32[]{:S(2)}) collective-permute-start(bf16[512,768]{1,0:T(8,128)(2,1)S(1)} %copy-done.46), channel_id=1, source_target_pairs={{0,16},{16,0},{8,24},{24,8},{1,17},{17,1},{9,25},{25,9},{2,18},{18... | collective-permute-start | bytes 2359304 | tf_op jit(solution)/shard_map/ppermute | solution.py:457
  90.8 16.8 %collective-permute-start.14 = (bf16[768,512]{1,0:T(8,128)(2,1)S(1)}, bf16[768,512]{1,0:T(8,128)(2,1)S(1)}, u32[]{:S(2)}, u32[]{:S(2)}) collective-permute-start(bf16[768,512]{1,0:T(8,128)(2,1)S(1)} %get-tuple-element.114), channel_id=1, source_target_pairs={{0,96},{32,0},{64,32},{96,64},{128,224},{160,128},{192,160},{224,1... | collective-permute-start | bytes 2359304 | tf_op jit(solution)/shard_map/ppermute | solution.py:459
  99.1 7.1 %copy-start.18 = (f32[512,1024]{1,0:T(8,128)S(1)}, f32[512,1024]{1,0:T(8,128)}, u32[]{:S(2)}) copy-start(f32[512,1024]{1,0:T(8,128)} %get-tuple-element.109.part_ref) | copy-start | bytes 6291460
  99.2 11.6 %collective-permute-start.15 = (bf16[512,768]{1,0:T(8,128)(2,1)S(1)}, bf16[512,768]{1,0:T(8,128)(2,1)S(1)}, u32[]{:S(2)}, u32[]{:S(2)}) collective-permute-start(bf16[512,768]{1,0:T(8,128)(2,1)S(1)} %mlp_part.2), channel_id=1, source_target_pairs={{0,8},{8,0},{16,24},{24,16},{1,9},{9,1},{17,25},{25,17},{2,10},{10... | collective-permute-start | bytes 2359304 | tf_op jit(solution)/shard_map/ppermute | solution.py:456
  113.1 11.4 %copy-start.2 = (bf16[768,2048]{1,0:T(8,128)(2,1)S(1)}, bf16[768,2048]{1,0:T(8,128)(2,1)}, u32[]{:S(2)}) copy-start(bf16[768,2048]{1,0:T(8,128)(2,1)} %g0.1) | copy-start | bytes 9437188
  113.1 11.4 %copy-start.4 = (bf16[768,2048]{1,0:T(8,128)(2,1)S(1)}, bf16[768,2048]{1,0:T(8,128)(2,1)}, u32[]{:S(2)}) copy-start(bf16[768,2048]{1,0:T(8,128)(2,1)} %u0.1) | copy-start | bytes 9437188
  118.2 9.9 %collective-permute-start.16 = (bf16[512,768]{1,0:T(8,128)(2,1)S(1)}, bf16[512,768]{1,0:T(8,128)(2,1)S(1)}, u32[]{:S(2)}, u32[]{:S(2)}) collective-permute-start(bf16[512,768]{1,0:T(8,128)(2,1)S(1)} %input_part.2), channel_id=1, source_target_pairs={{0,8},{8,0},{16,24},{24,16},{1,9},{9,1},{17,25},{25,17},{2,10},{10... | collective-permute-start | bytes 2359304 | tf_op jit(solution)/shard_map/ppermute | solution.py:456
  122.0 36.5 %collective-permute-start.20 = (bf16[1536,512]{1,0:T(8,128)(2,1)}, bf16[1536,512]{1,0:T(8,128)(2,1)}, u32[]{:S(2)}, u32[]{:S(2)}) collective-permute-start(bf16[1536,512]{1,0:T(8,128)(2,1)} %get-tuple-element.123), channel_id=1, source_target_pairs={{0,96},{32,0},{64,32},{96,64},{128,224},{160,128},{192,160},{224,1... | collective-permute-start | bytes 4718600 | tf_op jit(solution)/shard_map/ppermute | solution.py:459
  124.4 37.2 %collective-permute-start.19 = (bf16[1536,512]{1,0:T(8,128)(2,1)}, bf16[1536,512]{1,0:T(8,128)(2,1)}, u32[]{:S(2)}, u32[]{:S(2)}) collective-permute-start(bf16[1536,512]{1,0:T(8,128)(2,1)} %get-tuple-element.115), channel_id=1, source_target_pairs={{0,32},{32,64},{64,96},{96,0},{128,160},{160,192},{192,224},{224,1... | collective-permute-start | bytes 4718600 | tf_op jit(solution)/shard_map/ppermute | solution.py:458
  129.2 38.9 %all-to-all-start = ((bf16[8,64,768]{2,1,0:T(8,128)(2,1)}), bf16[8,64,768]{2,1,0:T(8,128)(2,1)S(1)}, u32[]{:S(2)}, u32[]{:S(2)}) async-start(bf16[8,64,768]{2,1,0:T(8,128)(2,1)} %bitcast.17), calls=%async_computation.1 | async-start | bytes 1572864 | tf_op jit(solution)/shard_map/all_to_all | solution.py:462
  137.3 70.2 %all-gather.2.cloned.1.call-start = ((), (), s32[]{:S(2)}) async-start(), calls=%async_computation.3 | async-start | bytes 1769472 | tf_op jit(solution)/shard_map/all_gather | solution.py:562
  137.3 5.4 %collective-permute-start.17 = (bf16[256,768]{1,0:T(8,128)(2,1)}, bf16[256,768]{1,0:T(8,128)(2,1)S(1)}, u32[]{:S(2)}, u32[]{:S(2)}) collective-permute-start(bf16[256,768]{1,0:T(8,128)(2,1)} %copy-done.44), channel_id=1, source_target_pairs={{0,8},{8,136},{16,24},{24,152},{32,40},{40,168},{48,56},{56,184},{... | collective-permute-start | bytes 1179656 | tf_op jit(solution)/shard_map/ppermute | solution.py:460
  137.7 12.3 %collective-permute-start.18 = (bf16[256,768]{1,0:T(8,128)(2,1)S(1)}, bf16[256,768]{1,0:T(8,128)(2,1)S(1)}, u32[]{:S(2)}, u32[]{:S(2)}) collective-permute-start(bf16[256,768]{1,0:T(8,128)(2,1)S(1)} %get-tuple-element.121), channel_id=1, source_target_pairs={{8,128},{24,144},{40,160},{56,176},{72,192},{88,208},{104,224},{12... | collective-permute-start | bytes 1179656 | tf_op jit(solution)/shard_map/ppermute | solution.py:461
  169.8 10.0 %collective-permute-start.21 = (bf16[768,512]{1,0:T(8,128)(2,1)}, bf16[768,512]{1,0:T(8,128)(2,1)S(1)}, u32[]{:S(2)}, u32[]{:S(2)}) collective-permute-start(bf16[768,512]{1,0:T(8,128)(2,1)} %copy-done.43), channel_id=1, source_target_pairs={{0,8},{8,136},{16,24},{24,152},{32,40},{40,168},{48,56},{56,184},{... | collective-permute-start | bytes 2359304 | tf_op jit(solution)/shard_map/ppermute | solution.py:460
  170.6 21.6 %collective-permute-start.22 = (bf16[768,512]{1,0:T(8,128)(2,1)}, bf16[768,512]{1,0:T(8,128)(2,1)S(1)}, u32[]{:S(2)}, u32[]{:S(2)}) collective-permute-start(bf16[768,512]{1,0:T(8,128)(2,1)} %copy-done.42), channel_id=1, source_target_pairs={{8,128},{24,144},{40,160},{56,176},{72,192},{88,208},{104,224},{12... | collective-permute-start | bytes 2359304 | tf_op jit(solution)/shard_map/ppermute | solution.py:461
  (41 other events, 111.1 us)
Sparse Core Ops, SparseCore 0:
  112.2 54.7 reduce-scatter.1
  170.0 37.4 all-gather.1

commit v2 on v1

--- a/solution.py
+++ b/solution.py
@@ -407,6 +407,43 @@
     )(mlp_sum, parts)
 
 
+def place_body(spot, mine_ref, *refs):
+    out_refs = refs[-2:]
+    height = mine_ref.shape[0]
+    feat = out_refs[0].shape[1]
+
+    def store(step, ref, low):
+        at = lax.rem(spot[2] + n_col + step, n_col) * height + low
+        for k, out_ref in enumerate(out_refs):
+            part = ref[:, k * feat : (k + 1) * feat]
+            out_ref[pl.ds(pl.multiple_of(at, ref.shape[0]), ref.shape[0]), :] = part
+
+    store(0, mine_ref, 0)
+    for j in range(3):
+        store(-1 - j, refs[j], 0)
+        store(1 + j, refs[3 + j], 0)
+    store(4, refs[6], 0)
+    store(4, refs[7], height // 2)
+
+
+def place(spot, *blocks):
+    height, both = blocks[0].shape
+    shape = jax.ShapeDtypeStruct((height * n_col, both // 2), bf16)
+    return pl.pallas_call(
+        place_body,
+        grid_spec=pltpu.PrefetchScalarGridSpec(
+            num_scalar_prefetch=1,
+            grid=(1,),
+            in_specs=[pl.BlockSpec(v.shape, lambda j, s: (0, 0)) for v in blocks],
+            out_specs=[pl.BlockSpec(shape.shape, lambda j, s: (0, 0))] * 2,
+        ),
+        out_shape=[shape, shape],
+        compiler_params=params(20),
+        cost_estimate=cost(1.5),
+        name="place",
+    )(spot, *blocks)
+
+
 def finish_body(spot, one_ref, keep_ref, two_ref, *out_refs):
     one = one_ref[...].astype(f32)
     n = out_refs[0].shape[2]
@@ -559,9 +596,18 @@
         spot, *tokens_t, grads_last, *gate_up_near,
     )
     gate_up_first, gate_up_second = home_one(first), home_two(second)
-    both = lax.all_gather(run(collect, mlp_sum, input_parts), "col", axis=0, tiled=True)
-    mlp_output, input_grad = both[:, :feat], both[:, feat:]
+    both = run(collect, mlp_sum, input_parts)
+    col_right = lambda value: lax.ppermute(value, "col", [(i, (i + 1) % n_col) for i in range(n_col)])
+    col_left = lambda value: lax.ppermute(value, "col", [(i, (i - 1) % n_col) for i in range(n_col)])
+    from_left, from_right = [col_right(both)], [col_left(both)]
+    for _ in range(2):
+        from_left.append(col_right(from_left[-1]))
+        from_right.append(col_left(from_right[-1]))
+    quarter = both.shape[0] // 2
+    end_left = col_right(from_left[-1][:quarter])
+    end_right = col_left(from_right[-1][quarter:])
     gate_out, up_out = run(functools.partial(finish, 2), spot, gate_up_first, gate_up_keep, gate_up_second)
+    mlp_output, input_grad = run(place, spot, both, *from_left, *from_right, end_left, end_right)
     return (mlp_output, input_grad, gate_out, up_out, down_out)
 
 

time: 221 us -> 215 us (0.973); the launches traced: 217 us -> 214 us
  waiting for transfers between devices: 73 us -> 58.4 us
  starting transfers between devices: 44.3 us -> 58.5 us
  local copies, waits for them, and re-layouts: 27.4 us -> 21.7 us
  Pallas kernels: 57 us -> 60.6 us
    ppermute x0 -> x8, starting transfers between devices: none -> 15.3 us  [the longest x4 15.2 us: local(): lax.ppermute(value, 'col', [(i, (i - 1) % n_col) for i in range(n_col)])]
    ppermute x0 -> x8, waiting for transfers between devices: none -> 13.7 us  [the longest x4 10.5 us: local(): lax.ppermute(value, 'col', [(i, (i - 1) % n_col) for i in range(n_col)])]
    ppermute x2, waiting for transfers between devices: 19.6 us -> 7.21 us  [local(): home_two = lambda value: lax.ppermute(value, ('depth', 'row'), home_second)]
    all_gather x1 -> x0, waiting for transfers between devices: 12 us -> none  [local(): lax.all_gather(run(collect, mlp_sum, input_parts), 'col', axis=0, tiled=T...]
    ppermute x2, waiting for transfers between devices: 5.57 us -> 1.17 us  [local(): home_one = lambda value: lax.ppermute(value, ('depth', 'row'), home_first)]
    unnamed x95 -> x91, local copies, waits for them, and re-layouts: 19 us -> 15.9 us
    slice x1 -> x2, local copies, waits for them, and re-layouts: 2.61 us -> 0.01 us  [the longest x1 0.01 us: local(): end_right = col_left(from_right[-1][quarter:])]
  transfers between devices with their start and end apart: 26 -> 33, of which waited for: 13 -> 17; matrix products, arithmetic and copies ran while one was open for 3% -> 3% of each run, Pallas kernels for 24% -> 25%
where the time goes in v2:
time: 215 us; the launch traced here: 214 us
  Pallas kernels  60.6 us (28%)
  starting transfers between devices  58.5 us (27%)
  waiting for transfers between devices  58.4 us (27%)
  local copies, waits for them, and re-layouts  21.7 us (10%)
  between operations  14.5 us (7%)
    ppermute x4, waiting for transfers between devices, local(): cross = lambda value: lax.ppermute(value, 'row', half_swap)  24.9 us
    unnamed x91, local copies, waits for them, and re-layouts  15.9 us
    ppermute x4, starting transfers between devices, local(): lax.ppermute(value, 'col', [(i, (i - 1) % n_col) for i in range(n_col)])  15.2 us
    pallas_call x4, Pallas kernels, activation_part(): pl.pallas_call(body, grid_spec=pltpu.PrefetchScalarGridSpec(num_scalar_pr...  13.2 us
    pallas_call x2, Pallas kernels, joint_partial(): pl.pallas_call(functools.partial(joint_body, gate_up_step, hg_steps), gri...  11.8 us
    pallas_call x2, Pallas kernels, gate_up_partial(): pl.pallas_call(gate_up_body, grid_spec=pltpu.PrefetchScalarGridSpec(num_s...  11.6 us
    ppermute x7, starting transfers between devices, local(): swap = lambda value: lax.ppermute(value, 'row', core_swap)  11.4 us
    ppermute x4, waiting for transfers between devices, local(): lax.ppermute(value, 'col', [(i, (i - 1) % n_col) for i in range(n_col)])  10.5 us
  transfers between devices with their start and end apart: 33, of which 17 were waited for; matrix products, arithmetic and copies ran while one was open for 3% of the time, Pallas kernels for 25%

profile of v2, /device:TPU:1, one launch (start us, length us, event | category | flops | bytes accessed | tf_op | source)
XLA Modules:
  0.0 214.3 jit_solution(4744451124828659840)
XLA Ops:
  8.6 3.3 %collective-permute-start = (bf16[512,768]{0,1:T(8,128)(2,1)S(1)}, bf16[512,768]{0,1:T(8,128)(2,1)S(1)}, u32[]{:S(2)}, u32[]{:S(2)}) collective-permute-start(bf16[512,768]{0,1:T(8,128)(2,1)S(1)} %copy.10), channel_id=1, source_target_pairs={{0,8},{8,0},{16,24},{24,16},{1,9},{9,1},{17,25},{25,17},{2,10},{10... | collective-permute-start | bytes 2359304 | tf_op jit(solution)/shard_map/ppermute | solution.py:493
  19.7 4.4 %gate_up_partial.2 = (f32[512,512]{1,0:T(8,128)}, bf16[512,512]{1,0:T(8,128)(2,1)}) custom-call(s32[4]{0:T(128)} %pad_add_fusion.spot, bf16[512,768]{1,0:T(8,128)(2,1)} %refs_0_.2, bf16[512,768]{1,0:T(8,128)(2,1)} %copy.11.oth_ref.refs_1_, bf16[768,2048]{1,0:T(8,128)(2,1)} %g0.1, bf16[768,2048]{1,0:T(8,128)(2,1)} %u0.1, ...), custom_call_target="tpu_custom_call" | custom-call | flops 1 | bytes 14850000 | tf_op jit(solution)/shard_map/gate_up_partial/pallas_call | solution.py:98
  27.1 7.2 %gate_up_partial.3 = (f32[512,1024]{1,0:T(8,128)}, bf16[512,1024]{1,0:T(8,128)(2,1)}) custom-call(s32[4]{0:T(128)} %pad_add_fusion.spot, bf16[512,768]{1,0:T(8,128)(2,1)} %refs_0_.2, bf16[512,768]{1,0:T(8,128)(2,1)} %copy.11.oth_ref.refs_1_, bf16[768,2048]{1,0:T(8,128)(2,1)} %g0.1, bf16[768,2048]{1,0:T(8,128)(2,1)} %u0.1, ...), custom_call_target="tpu_custom_call" | custom-call | flops 1 | bytes 14850000 | tf_op jit(solution)/shard_map/gate_up_partial/pallas_call | solution.py:98
  34.4 4.9 %collective-permute-done.3.got_ref = bf16[512,512]{1,0:T(8,128)(2,1)S(1)} collective-permute-done((bf16[512,512]{1,0:T(8,128)(2,1)}, bf16[512,512]{1,0:T(8,128)(2,1)S(1)}, u32[]{:S(2)}, u32[]{:S(2)}) %collective-permute-start.3) | collective-permute-done | bytes 524320 | tf_op jit(solution)/shard_map/ppermute | solution.py:494
  42.0 2.5 %collective-permute-start.8 = (bf16[256,768]{1,0:T(8,128)(2,1)S(1)}, bf16[256,768]{1,0:T(8,128)(2,1)S(1)}, u32[]{:S(2)}, u32[]{:S(2)}) collective-permute-start(bf16[256,768]{1,0:T(8,128)(2,1)S(1)} %get-tuple-element.92), channel_id=1, source_target_pairs={{0,96},{32,0},{64,32},{96,64},{128,224},{160,128},{192,160},{224,1... | collective-permute-start | bytes 1179656 | tf_op jit(solution)/shard_map/ppermute | solution.py:496
  45.6 6.1 %joint_partial.2 = (f32[512,512]{1,0:T(8,128)}, f32[512,256]{1,0:T(8,128)}, bf16[512,768]{1,0:T(8,128)(2,1)}) custom-call(s32[4]{0:T(128)} %pad_add_fusion.spot, bf16[512,768]{1,0:T(8,128)(2,1)} %refs_0_.2, bf16[512,768]{1,0:T(8,128)(2,1)} %copy.11.oth_ref.refs_1_, bf16[768,2048]{1,0:T(8,128)(2,1)} %g0.1, bf16[768,2048]{1,0:T(8,128)(2,1)} %u0.1, ...), custom_call_target="tpu_custom_call" | custom-call | flops 1 | bytes 19800000 | tf_op jit(solution)/shard_map/joint_partial/pallas_call | solution.py:156
  51.8 12.9 %collective-permute-done.6.got_ref = bf16[512,1024]{1,0:T(8,128)(2,1)S(1)} collective-permute-done((bf16[512,1024]{1,0:T(8,128)(2,1)}, bf16[512,1024]{1,0:T(8,128)(2,1)S(1)}, u32[]{:S(2)}, u32[]{:S(2)}) %collective-permute-start.6) | collective-permute-done | bytes 1048608 | tf_op jit(solution)/shard_map/ppermute | solution.py:494
  69.4 2.3 %collective-permute-start.11 = (bf16[512,768]{1,0:T(8,128)(2,1)}, bf16[512,768]{1,0:T(8,128)(2,1)}, u32[]{:S(2)}, u32[]{:S(2)}) collective-permute-start(bf16[512,768]{1,0:T(8,128)(2,1)} %get-tuple-element.108), channel_id=1, source_target_pairs={{0,96},{32,0},{64,32},{96,64},{128,224},{160,128},{192,160},{224,1... | collective-permute-start | bytes 2359304 | tf_op jit(solution)/shard_map/ppermute | solution.py:496
  71.8 5.7 %joint_partial.3 = (f32[512,768]{1,0:T(8,128)}, bf16[512,768]{1,0:T(8,128)(2,1)}) custom-call(s32[4]{0:T(128)} %pad_add_fusion.spot, bf16[512,768]{1,0:T(8,128)(2,1)} %b0.5, bf16[512,768]{1,0:T(8,128)(2,1)} %copy-done.10, bf16[2048,768]{1,0:T(8,128)(2,1)} %w0.1, bf16[1024,768]{1,0:T(8,128)(2,1)} %copy-done.5, bf16[2048,768]{1,0:T(8,128)(2,1)} %w0.1, ...), custom_call_target="tpu_custom_call" | custom-call | flops 1 | bytes 19800000 | tf_op jit(solution)/shard_map/joint_partial/pallas_call | solution.py:156
  77.7 5.9 %collective-permute-done.9.hg_got_ref.got_ref = bf16[512,768]{1,0:T(8,128)(2,1)S(1)} collective-permute-done((bf16[512,768]{1,0:T(8,128)(2,1)}, bf16[512,768]{1,0:T(8,128)(2,1)S(1)}, u32[]{:S(2)}, u32[]{:S(2)}) %collective-permute-start.9) | collective-permute-done | bytes 786464 | tf_op jit(solution)/shard_map/ppermute | solution.py:494
  92.5 2.7 %last_terms.2 = (f32[256,768]{1,0:T(8,128)S(1)}, bf16[256,768]{1,0:T(8,128)(2,1)S(1)}, bf16[256,768]{1,0:T(8,128)(2,1)S(1)}) custom-call(s32[4]{0:T(128)S(1)} %copy-done.41, bf16[256,512]{1,0:T(8,128)(2,1)S(1)} %get-tuple-element.107.a0.a1, bf16[256,512]{1,0:T(8,128)(2,1)S(1)} %get-tuple-element.107.a0.a1, bf16[512,768]{1,0:T(8,128)(2,1)S(1)} %copy-done.9, ...), custom_call_target="tpu_custom_call" | custom-call | flops 1 | bytes 4290000 | tf_op jit(solution)/shard_map/last_terms/pallas_call | solution.py:371
  99.1 3.6 %collective-permute-start.15 = (bf16[512,768]{1,0:T(8,128)(2,1)S(1)}, bf16[512,768]{1,0:T(8,128)(2,1)S(1)}, u32[]{:S(2)}, u32[]{:S(2)}) collective-permute-start(bf16[512,768]{1,0:T(8,128)(2,1)S(1)} %mlp_part.2), channel_id=1, source_target_pairs={{0,8},{8,0},{16,24},{24,16},{1,9},{9,1},{17,25},{25,17},{2,10},{10... | collective-permute-start | bytes 2359304 | tf_op jit(solution)/shard_map/ppermute | solution.py:493
  107.6 3.1 %near_terms.3 = (bf16[1536,512]{1,0:T(8,128)(2,1)}, bf16[1536,512]{1,0:T(8,128)(2,1)}) custom-call(bf16[768,512]{1,0:T(8,128)(2,1)S(1)} %bitcast.13, bf16[768,512]{1,0:T(8,128)(2,1)S(1)} %bitcast.9, bf16[768,512]{1,0:T(8,128)(2,1)S(1)} %bitcast.14, bf16[768,512]{1,0:T(8,128)(2,1)S(1)} %bitcast.10, bf16[512,1024]{1,0:T(8,128)(2,1)S(1)} %grads_step.4.b0.b1.d0.d1.near_ref, ...), custom_call_target="tpu_custom_call" | custom-call | flops 1 | bytes 7260000 | tf_op jit(solution)/shard_map/near_terms/pallas_call | solution.py:340
  113.1 5.1 %input_part.2 = bf16[512,768]{1,0:T(8,128)(2,1)S(1)} custom-call(s32[4]{0:T(128)S(1)} %copy-done.41, bf16[512,512]{1,0:T(8,128)(2,1)S(1)} %copy-done.16, bf16[512,1024]{1,0:T(8,128)(2,1)S(1)} %grads_step.4.b0.b1.d0.d1.near_ref, bf16[512,512]{1,0:T(8,128)(2,1)S(1)} %grads_step.5.last_ref.b0.b1, ...), custom_call_target="tpu_custom_call" | custom-call | flops 1 | bytes 8250000 | tf_op jit(solution)/shard_map/input_part/pallas_call | solution.py:262
  118.2 3.8 %collective-permute-start.16 = (bf16[512,768]{1,0:T(8,128)(2,1)S(1)}, bf16[512,768]{1,0:T(8,128)(2,1)S(1)}, u32[]{:S(2)}, u32[]{:S(2)}) collective-permute-start(bf16[512,768]{1,0:T(8,128)(2,1)S(1)} %input_part.2), channel_id=1, source_target_pairs={{0,8},{8,0},{16,24},{24,16},{1,9},{9,1},{17,25},{25,17},{2,10},{10... | collective-permute-start | bytes 2359304 | tf_op jit(solution)/shard_map/ppermute | solution.py:493
  122.0 2.5 %collective-permute-start.20 = (bf16[1536,512]{1,0:T(8,128)(2,1)}, bf16[1536,512]{1,0:T(8,128)(2,1)}, u32[]{:S(2)}, u32[]{:S(2)}) collective-permute-start(bf16[1536,512]{1,0:T(8,128)(2,1)} %get-tuple-element.126), channel_id=1, source_target_pairs={{0,96},{32,0},{64,32},{96,64},{128,224},{160,128},{192,160},{224,1... | collective-permute-start | bytes 4718600 | tf_op jit(solution)/shard_map/ppermute | solution.py:496
  124.5 3.6 %input_part.3.own_ref = f32[512,768]{1,0:T(8,128)S(1)} custom-call(s32[4]{0:T(128)S(1)} %copy-done.41, bf16[512,512]{1,0:T(8,128)(2,1)S(1)} %copy-done.16, bf16[512,1024]{1,0:T(8,128)(2,1)S(1)} %grads_step.4.b0.b1.d0.d1.near_ref, bf16[512,512]{1,0:T(8,128)(2,1)S(1)} %grads_step.5.last_ref.b0.b1, bf16[768,2048]{1,0:T(8,128)(2,1)S(1)} %copy-done.2, ...), custom_call_target="tpu_custom_call" | custom-call | flops 1 | bytes 8250000 | tf_op jit(solution)/shard_map/input_part/pallas_call | solution.py:262
  129.2 8.0 %all-to-all-start = ((bf16[8,64,768]{2,1,0:T(8,128)(2,1)}), bf16[8,64,768]{2,1,0:T(8,128)(2,1)S(1)}, u32[]{:S(2)}, u32[]{:S(2)}) async-start(bf16[8,64,768]{2,1,0:T(8,128)(2,1)} %bitcast.17), calls=%async_computation.1 | async-start | bytes 1572864 | tf_op jit(solution)/shard_map/all_to_all | solution.py:499
  137.5 3.9 %collective-permute-start.18 = (bf16[256,768]{1,0:T(8,128)(2,1)S(1)}, bf16[256,768]{1,0:T(8,128)(2,1)S(1)}, u32[]{:S(2)}, u32[]{:S(2)}) collective-permute-start(bf16[256,768]{1,0:T(8,128)(2,1)S(1)} %get-tuple-element.124), channel_id=1, source_target_pairs={{8,128},{24,144},{40,160},{56,176},{72,192},{88,208},{104,224},{12... | collective-permute-start | bytes 1179656 | tf_op jit(solution)/shard_map/ppermute | solution.py:498
  142.6 7.2 %collective-permute-done.18.two_ref = bf16[256,768]{1,0:T(8,128)(2,1)S(1)} collective-permute-done((bf16[256,768]{1,0:T(8,128)(2,1)S(1)}, bf16[256,768]{1,0:T(8,128)(2,1)S(1)}, u32[]{:S(2)}, u32[]{:S(2)}) %collective-permute-start.18) | collective-permute-done | bytes 393248 | tf_op jit(solution)/shard_map/ppermute | solution.py:498
  152.5 6.0 %collective-permute-done.20.from_right = bf16[1536,512]{1,0:T(8,128)(2,1)} collective-permute-done((bf16[1536,512]{1,0:T(8,128)(2,1)}, bf16[1536,512]{1,0:T(8,128)(2,1)}, u32[]{:S(2)}, u32[]{:S(2)}) %collective-permute-start.20) | collective-permute-done | bytes 1572896 | tf_op jit(solution)/shard_map/ppermute | solution.py:496
  158.5 3.1 %collective-permute-done.19.from_left = bf16[1536,512]{1,0:T(8,128)(2,1)} collective-permute-done((bf16[1536,512]{1,0:T(8,128)(2,1)}, bf16[1536,512]{1,0:T(8,128)(2,1)}, u32[]{:S(2)}, u32[]{:S(2)}) %collective-permute-start.19) | collective-permute-done | bytes 1572896 | tf_op jit(solution)/shard_map/ppermute | solution.py:495
  161.6 4.7 %last_terms.3 = (f32[768,512]{1,0:T(8,128)S(1)}, bf16[768,512]{1,0:T(8,128)(2,1)}, bf16[768,512]{1,0:T(8,128)(2,1)}) custom-call(s32[4]{0:T(128)S(1)} %copy-done.41, bf16[768,512]{1,0:T(8,128)(2,1)S(1)} %bitcast.15, bf16[768,512]{1,0:T(8,128)(2,1)S(1)} %bitcast.11, bf16[512,512]{1,0:T(8,128)(2,1)S(1)} %grads_step.5.last_ref.b0.b1, ...), custom_call_target="tpu_custom_call" | custom-call | flops 1 | bytes 4290000 | tf_op jit(solution)/shard_map/last_terms/pallas_call | solution.py:371
  167.6 4.6 %collective-permute-start.22 = (bf16[768,512]{1,0:T(8,128)(2,1)}, bf16[768,512]{1,0:T(8,128)(2,1)}, u32[]{:S(2)}, u32[]{:S(2)}) collective-permute-start(bf16[768,512]{1,0:T(8,128)(2,1)} %get-tuple-element.131), channel_id=1, source_target_pairs={{8,128},{24,144},{40,160},{56,176},{72,192},{88,208},{104,224},{12... | collective-permute-start | bytes 2359304 | tf_op jit(solution)/shard_map/ppermute | solution.py:498
  173.3 5.5 %collective-permute-start.26 = (bf16[64,1536]{1,0:T(8,128)(2,1)S(1)}, bf16[64,1536]{1,0:T(8,128)(2,1)S(1)}, u32[]{:S(2)}, u32[]{:S(2)}) collective-permute-start(bf16[64,1536]{1,0:T(8,128)(2,1)S(1)} %collect.1.mine_ref), channel_id=1, source_target_pairs={{0,7},{1,0},{2,1},{3,2},{4,3},{5,4},{6,5},{7,6},{8,15},{9,8},{10,9... | collective-permute-start | bytes 589832 | tf_op jit(solution)/shard_map/ppermute | solution.py:601
  178.8 3.3 %collective-permute-done.26.refs_3_ = bf16[64,1536]{1,0:T(8,128)(2,1)S(1)} collective-permute-done((bf16[64,1536]{1,0:T(8,128)(2,1)S(1)}, bf16[64,1536]{1,0:T(8,128)(2,1)S(1)}, u32[]{:S(2)}, u32[]{:S(2)}) %collective-permute-start.26) | collective-permute-done | bytes 196640 | tf_op jit(solution)/shard_map/ppermute | solution.py:601
  182.1 3.1 %collective-permute-start.27 = (bf16[64,1536]{1,0:T(8,128)(2,1)S(1)}, bf16[64,1536]{1,0:T(8,128)(2,1)S(1)}, u32[]{:S(2)}, u32[]{:S(2)}) collective-permute-start(bf16[64,1536]{1,0:T(8,128)(2,1)S(1)} %collective-permute-done.26.refs_3_), channel_id=1, source_target_pairs={{0,7},{1,0},{2,1},{3,2},{4,3},{5,4},{6,5},{7,6},{8,15},{9,8},{10,9... | collective-permute-start | bytes 589832 | tf_op jit(solution)/shard_map/ppermute | solution.py:601
  185.5 4.2 %collective-permute-done.27.refs_4_ = bf16[64,1536]{1,0:T(8,128)(2,1)S(1)} collective-permute-done((bf16[64,1536]{1,0:T(8,128)(2,1)S(1)}, bf16[64,1536]{1,0:T(8,128)(2,1)S(1)}, u32[]{:S(2)}, u32[]{:S(2)}) %collective-permute-start.27) | collective-permute-done | bytes 196640 | tf_op jit(solution)/shard_map/ppermute | solution.py:601
  189.7 3.1 %collective-permute-start.28 = (bf16[64,1536]{1,0:T(8,128)(2,1)S(1)}, bf16[64,1536]{1,0:T(8,128)(2,1)S(1)}, u32[]{:S(2)}, u32[]{:S(2)}) collective-permute-start(bf16[64,1536]{1,0:T(8,128)(2,1)S(1)} %collective-permute-done.27.refs_4_), channel_id=1, source_target_pairs={{0,7},{1,0},{2,1},{3,2},{4,3},{5,4},{6,5},{7,6},{8,15},{9,8},{10,9... | collective-permute-start | bytes 589832 | tf_op jit(solution)/shard_map/ppermute | solution.py:601
  193.6 3.1 %collective-permute-done.28.refs_5_ = bf16[64,1536]{1,0:T(8,128)(2,1)S(1)} collective-permute-done((bf16[64,1536]{1,0:T(8,128)(2,1)S(1)}, bf16[64,1536]{1,0:T(8,128)(2,1)S(1)}, u32[]{:S(2)}, u32[]{:S(2)}) %collective-permute-start.28) | collective-permute-done | bytes 196640 | tf_op jit(solution)/shard_map/ppermute | solution.py:601
  196.7 3.5 %collective-permute-start.30 = (bf16[32,1536]{1,0:T(8,128)(2,1)S(1)}, bf16[32,1536]{1,0:T(8,128)(2,1)S(1)}, u32[]{:S(2)}, u32[]{:S(2)}) collective-permute-start(bf16[32,1536]{1,0:T(8,128)(2,1)S(1)} %slice.9), channel_id=1, source_target_pairs={{0,7},{1,0},{2,1},{3,2},{4,3},{5,4},{6,5},{7,6},{8,15},{9,8},{10,9... | collective-permute-start | bytes 294920 | tf_op jit(solution)/shard_map/ppermute | solution.py:601
  201.0 3.3 %finish.3 = (f32[1,768,256]{2,1,0:T(8,128)}, f32[1,768,256]{2,1,0:T(8,128)}) custom-call(s32[4]{0:T(128)S(1)} %copy-done.41, bf16[768,512]{1,0:T(8,128)(2,1)} %collective-permute-done.21.one_ref, f32[768,512]{1,0:T(8,128)S(1)} %copy-done.34, bf16[768,512]{1,0:T(8,128)(2,1)} %collective-permute-done.22.two_ref), custom_call_target="tpu_custom_call" | custom-call | flops 1 | bytes 4950000 | tf_op jit(solution)/shard_map/finish/pallas_call | solution.py:468
  (160 shorter events, 53.5 us)
Async XLA Ops:
  7.2 165.1 %reduce-scatter.2.cloned.1.call-start = ((), (), s32[]{:S(2)}) async-start(), calls=%async_computation.2 | async-start | bytes 1769472 | tf_op jit(solution)/shard_map/reduce_scatter | solution.py:581
  8.6 5.2 %collective-permute-start = (bf16[512,768]{0,1:T(8,128)(2,1)S(1)}, bf16[512,768]{0,1:T(8,128)(2,1)S(1)}, u32[]{:S(2)}, u32[]{:S(2)}) collective-permute-start(bf16[512,768]{0,1:T(8,128)(2,1)S(1)} %copy.10), channel_id=1, source_target_pairs={{0,8},{8,0},{16,24},{24,16},{1,9},{9,1},{17,25},{25,17},{2,10},{10... | collective-permute-start | bytes 2359304 | tf_op jit(solution)/shard_map/ppermute | solution.py:493
  15.7 4.0 %collective-permute-start.2 = (bf16[768,1024]{1,0:T(8,128)(2,1)}, bf16[768,1024]{1,0:T(8,128)(2,1)}, u32[]{:S(2)}, u32[]{:S(2)}) collective-permute-start(bf16[768,1024]{1,0:T(8,128)(2,1)} %constant_dynamic-slice_fusion.1), channel_id=1, source_target_pairs={{0,8},{8,0},{16,24},{24,16},{1,9},{9,1},{17,25},{25,17},{2,10},{10... | collective-permute-start | bytes 4718600 | tf_op jit(solution)/shard_map/ppermute | solution.py:493
  24.1 15.2 %collective-permute-start.3 = (bf16[512,512]{1,0:T(8,128)(2,1)}, bf16[512,512]{1,0:T(8,128)(2,1)S(1)}, u32[]{:S(2)}, u32[]{:S(2)}) collective-permute-start(bf16[512,512]{1,0:T(8,128)(2,1)} %get-tuple-element.79), channel_id=1, source_target_pairs={{0,16},{16,0},{8,24},{24,8},{1,17},{17,1},{9,25},{25,9},{2,18},{18... | collective-permute-start | bytes 1572872 | tf_op jit(solution)/shard_map/ppermute | solution.py:494
  26.6 17.8 %collective-permute-start.5 = (bf16[1024,768]{1,0:T(8,128)(2,1)}, bf16[1024,768]{1,0:T(8,128)(2,1)S(1)}, u32[]{:S(2)}, u32[]{:S(2)}) collective-permute-start(bf16[1024,768]{1,0:T(8,128)(2,1)} %constant_dynamic-slice_fusion), channel_id=1, source_target_pairs={{0,8},{8,0},{16,24},{24,16},{1,9},{9,1},{17,25},{25,17},{2,10},{10... | collective-permute-start | bytes 4718600 | tf_op jit(solution)/shard_map/ppermute | solution.py:493
  27.0 14.3 %collective-permute-start.4 = (bf16[512,768]{1,0:T(8,128)(2,1)S(1)}, bf16[512,768]{1,0:T(8,128)(2,1)S(1)}, u32[]{:S(2)}, u32[]{:S(2)}) collective-permute-start(bf16[512,768]{1,0:T(8,128)(2,1)S(1)} %copy-done.7), channel_id=1, source_target_pairs={{0,8},{8,0},{16,24},{24,16},{1,9},{9,1},{17,25},{25,17},{2,10},{10... | collective-permute-start | bytes 2359304 | tf_op jit(solution)/shard_map/ppermute | solution.py:493
  39.3 25.4 %collective-permute-start.6 = (bf16[512,1024]{1,0:T(8,128)(2,1)}, bf16[512,1024]{1,0:T(8,128)(2,1)S(1)}, u32[]{:S(2)}, u32[]{:S(2)}) collective-permute-start(bf16[512,1024]{1,0:T(8,128)(2,1)} %get-tuple-element.88), channel_id=1, source_target_pairs={{0,16},{16,0},{8,24},{24,8},{1,17},{17,1},{9,25},{25,9},{2,18},{18... | collective-permute-start | bytes 3145736 | tf_op jit(solution)/shard_map/ppermute | solution.py:494
  42.0 25.5 %collective-permute-start.8 = (bf16[256,768]{1,0:T(8,128)(2,1)S(1)}, bf16[256,768]{1,0:T(8,128)(2,1)S(1)}, u32[]{:S(2)}, u32[]{:S(2)}) collective-permute-start(bf16[256,768]{1,0:T(8,128)(2,1)S(1)} %get-tuple-element.92), channel_id=1, source_target_pairs={{0,96},{32,0},{64,32},{96,64},{128,224},{160,128},{192,160},{224,1... | collective-permute-start | bytes 1179656 | tf_op jit(solution)/shard_map/ppermute | solution.py:496
  44.5 23.0 %collective-permute-start.7 = (bf16[256,768]{1,0:T(8,128)(2,1)S(1)}, bf16[256,768]{1,0:T(8,128)(2,1)S(1)}, u32[]{:S(2)}, u32[]{:S(2)}) collective-permute-start(bf16[256,768]{1,0:T(8,128)(2,1)S(1)} %get-tuple-element.83), channel_id=1, source_target_pairs={{0,32},{32,64},{64,96},{96,0},{128,160},{160,192},{192,224},{224,1... | collective-permute-start | bytes 1179656 | tf_op jit(solution)/shard_map/ppermute | solution.py:495
  64.7 18.9 %collective-permute-start.9 = (bf16[512,768]{1,0:T(8,128)(2,1)}, bf16[512,768]{1,0:T(8,128)(2,1)S(1)}, u32[]{:S(2)}, u32[]{:S(2)}) collective-permute-start(bf16[512,768]{1,0:T(8,128)(2,1)} %get-tuple-element.101), channel_id=1, source_target_pairs={{0,16},{16,0},{8,24},{24,8},{1,17},{17,1},{9,25},{25,9},{2,18},{18... | collective-permute-start | bytes 2359304 | tf_op jit(solution)/shard_map/ppermute | solution.py:494
  69.4 23.1 %collective-permute-start.11 = (bf16[512,768]{1,0:T(8,128)(2,1)}, bf16[512,768]{1,0:T(8,128)(2,1)}, u32[]{:S(2)}, u32[]{:S(2)}) collective-permute-start(bf16[512,768]{1,0:T(8,128)(2,1)} %get-tuple-element.108), channel_id=1, source_target_pairs={{0,96},{32,0},{64,32},{96,64},{128,224},{160,128},{192,160},{224,1... | collective-permute-start | bytes 2359304 | tf_op jit(solution)/shard_map/ppermute | solution.py:496
  71.8 20.7 %collective-permute-start.10 = (bf16[512,768]{1,0:T(8,128)(2,1)}, bf16[512,768]{1,0:T(8,128)(2,1)}, u32[]{:S(2)}, u32[]{:S(2)}) collective-permute-start(bf16[512,768]{1,0:T(8,128)(2,1)} %get-tuple-element.93), channel_id=1, source_target_pairs={{0,32},{32,64},{64,96},{96,0},{128,160},{160,192},{192,224},{224,1... | collective-permute-start | bytes 2359304 | tf_op jit(solution)/shard_map/ppermute | solution.py:495
  88.1 19.5 %collective-permute-start.13 = (bf16[768,512]{1,0:T(8,128)(2,1)S(1)}, bf16[768,512]{1,0:T(8,128)(2,1)S(1)}, u32[]{:S(2)}, u32[]{:S(2)}) collective-permute-start(bf16[768,512]{1,0:T(8,128)(2,1)S(1)} %get-tuple-element.103), channel_id=1, source_target_pairs={{0,32},{32,64},{64,96},{96,0},{128,160},{160,192},{192,224},{224,1... | collective-permute-start | bytes 2359304 | tf_op jit(solution)/shard_map/ppermute | solution.py:495
  88.4 17.8 %collective-permute-start.12 = (bf16[512,768]{1,0:T(8,128)(2,1)S(1)}, bf16[512,768]{1,0:T(8,128)(2,1)S(1)}, u32[]{:S(2)}, u32[]{:S(2)}) collective-permute-start(bf16[512,768]{1,0:T(8,128)(2,1)S(1)} %copy-done.44), channel_id=1, source_target_pairs={{0,16},{16,0},{8,24},{24,8},{1,17},{17,1},{9,25},{25,9},{2,18},{18... | collective-permute-start | bytes 2359304 | tf_op jit(solution)/shard_map/ppermute | solution.py:494
  90.8 16.8 %collective-permute-start.14 = (bf16[768,512]{1,0:T(8,128)(2,1)S(1)}, bf16[768,512]{1,0:T(8,128)(2,1)S(1)}, u32[]{:S(2)}, u32[]{:S(2)}) collective-permute-start(bf16[768,512]{1,0:T(8,128)(2,1)S(1)} %get-tuple-element.117), channel_id=1, source_target_pairs={{0,96},{32,0},{64,32},{96,64},{128,224},{160,128},{192,160},{224,1... | collective-permute-start | bytes 2359304 | tf_op jit(solution)/shard_map/ppermute | solution.py:496
  99.1 11.6 %collective-permute-start.15 = (bf16[512,768]{1,0:T(8,128)(2,1)S(1)}, bf16[512,768]{1,0:T(8,128)(2,1)S(1)}, u32[]{:S(2)}, u32[]{:S(2)}) collective-permute-start(bf16[512,768]{1,0:T(8,128)(2,1)S(1)} %mlp_part.2), channel_id=1, source_target_pairs={{0,8},{8,0},{16,24},{24,16},{1,9},{9,1},{17,25},{25,17},{2,10},{10... | collective-permute-start | bytes 2359304 | tf_op jit(solution)/shard_map/ppermute | solution.py:493
  118.2 9.9 %collective-permute-start.16 = (bf16[512,768]{1,0:T(8,128)(2,1)S(1)}, bf16[512,768]{1,0:T(8,128)(2,1)S(1)}, u32[]{:S(2)}, u32[]{:S(2)}) collective-permute-start(bf16[512,768]{1,0:T(8,128)(2,1)S(1)} %input_part.2), channel_id=1, source_target_pairs={{0,8},{8,0},{16,24},{24,16},{1,9},{9,1},{17,25},{25,17},{2,10},{10... | collective-permute-start | bytes 2359304 | tf_op jit(solution)/shard_map/ppermute | solution.py:493
  122.0 36.5 %collective-permute-start.20 = (bf16[1536,512]{1,0:T(8,128)(2,1)}, bf16[1536,512]{1,0:T(8,128)(2,1)}, u32[]{:S(2)}, u32[]{:S(2)}) collective-permute-start(bf16[1536,512]{1,0:T(8,128)(2,1)} %get-tuple-element.126), channel_id=1, source_target_pairs={{0,96},{32,0},{64,32},{96,64},{128,224},{160,128},{192,160},{224,1... | collective-permute-start | bytes 4718600 | tf_op jit(solution)/shard_map/ppermute | solution.py:496
  124.5 37.2 %collective-permute-start.19 = (bf16[1536,512]{1,0:T(8,128)(2,1)}, bf16[1536,512]{1,0:T(8,128)(2,1)}, u32[]{:S(2)}, u32[]{:S(2)}) collective-permute-start(bf16[1536,512]{1,0:T(8,128)(2,1)} %get-tuple-element.118), channel_id=1, source_target_pairs={{0,32},{32,64},{64,96},{96,0},{128,160},{160,192},{192,224},{224,1... | collective-permute-start | bytes 4718600 | tf_op jit(solution)/shard_map/ppermute | solution.py:495
  129.2 43.0 %all-to-all-start = ((bf16[8,64,768]{2,1,0:T(8,128)(2,1)}), bf16[8,64,768]{2,1,0:T(8,128)(2,1)S(1)}, u32[]{:S(2)}, u32[]{:S(2)}) async-start(bf16[8,64,768]{2,1,0:T(8,128)(2,1)} %bitcast.17), calls=%async_computation.1 | async-start | bytes 1572864 | tf_op jit(solution)/shard_map/all_to_all | solution.py:499
  137.2 5.3 %collective-permute-start.17 = (bf16[256,768]{1,0:T(8,128)(2,1)}, bf16[256,768]{1,0:T(8,128)(2,1)S(1)}, u32[]{:S(2)}, u32[]{:S(2)}) collective-permute-start(bf16[256,768]{1,0:T(8,128)(2,1)} %copy-done.42), channel_id=1, source_target_pairs={{0,8},{8,136},{16,24},{24,152},{32,40},{40,168},{48,56},{56,184},{... | collective-permute-start | bytes 1179656 | tf_op jit(solution)/shard_map/ppermute | solution.py:497
  137.5 12.2 %collective-permute-start.18 = (bf16[256,768]{1,0:T(8,128)(2,1)S(1)}, bf16[256,768]{1,0:T(8,128)(2,1)S(1)}, u32[]{:S(2)}, u32[]{:S(2)}) collective-permute-start(bf16[256,768]{1,0:T(8,128)(2,1)S(1)} %get-tuple-element.124), channel_id=1, source_target_pairs={{8,128},{24,144},{40,160},{56,176},{72,192},{88,208},{104,224},{12... | collective-permute-start | bytes 1179656 | tf_op jit(solution)/shard_map/ppermute | solution.py:498
  167.5 33.5 %collective-permute-start.21 = (bf16[768,512]{1,0:T(8,128)(2,1)}, bf16[768,512]{1,0:T(8,128)(2,1)}, u32[]{:S(2)}, u32[]{:S(2)}) collective-permute-start(bf16[768,512]{1,0:T(8,128)(2,1)} %get-tuple-element.130), channel_id=1, source_target_pairs={{0,8},{8,136},{16,24},{24,152},{32,40},{40,168},{48,56},{56,184},{... | collective-permute-start | bytes 2359304 | tf_op jit(solution)/shard_map/ppermute | solution.py:497
  167.6 33.4 %collective-permute-start.22 = (bf16[768,512]{1,0:T(8,128)(2,1)}, bf16[768,512]{1,0:T(8,128)(2,1)}, u32[]{:S(2)}, u32[]{:S(2)}) collective-permute-start(bf16[768,512]{1,0:T(8,128)(2,1)} %get-tuple-element.131), channel_id=1, source_target_pairs={{8,128},{24,144},{40,160},{56,176},{72,192},{88,208},{104,224},{12... | collective-permute-start | bytes 2359304 | tf_op jit(solution)/shard_map/ppermute | solution.py:498
  173.3 8.8 %collective-permute-start.26 = (bf16[64,1536]{1,0:T(8,128)(2,1)S(1)}, bf16[64,1536]{1,0:T(8,128)(2,1)S(1)}, u32[]{:S(2)}, u32[]{:S(2)}) collective-permute-start(bf16[64,1536]{1,0:T(8,128)(2,1)S(1)} %collect.1.mine_ref), channel_id=1, source_target_pairs={{0,7},{1,0},{2,1},{3,2},{4,3},{5,4},{6,5},{7,6},{8,15},{9,8},{10,9... | collective-permute-start | bytes 589832 | tf_op jit(solution)/shard_map/ppermute | solution.py:601
  178.8 6.7 %collective-permute-start.23 = (bf16[64,1536]{1,0:T(8,128)(2,1)S(1)}, bf16[64,1536]{1,0:T(8,128)(2,1)S(1)}, u32[]{:S(2)}, u32[]{:S(2)}) collective-permute-start(bf16[64,1536]{1,0:T(8,128)(2,1)S(1)} %collect.1.mine_ref), channel_id=1, source_target_pairs={{0,1},{1,2},{2,3},{3,4},{4,5},{5,6},{6,7},{7,0},{8,9},{9,10},{10,1... | collective-permute-start | bytes 589832 | tf_op jit(solution)/shard_map/ppermute | solution.py:600
  182.1 7.5 %collective-permute-start.27 = (bf16[64,1536]{1,0:T(8,128)(2,1)S(1)}, bf16[64,1536]{1,0:T(8,128)(2,1)S(1)}, u32[]{:S(2)}, u32[]{:S(2)}) collective-permute-start(bf16[64,1536]{1,0:T(8,128)(2,1)S(1)} %collective-permute-done.26.refs_3_), channel_id=1, source_target_pairs={{0,7},{1,0},{2,1},{3,2},{4,3},{5,4},{6,5},{7,6},{8,15},{9,8},{10,9... | collective-permute-start | bytes 589832 | tf_op jit(solution)/shard_map/ppermute | solution.py:601
  185.5 8.1 %collective-permute-start.24 = (bf16[64,1536]{1,0:T(8,128)(2,1)S(1)}, bf16[64,1536]{1,0:T(8,128)(2,1)S(1)}, u32[]{:S(2)}, u32[]{:S(2)}) collective-permute-start(bf16[64,1536]{1,0:T(8,128)(2,1)S(1)} %collective-permute-done.23.refs_0_), channel_id=1, source_target_pairs={{0,1},{1,2},{2,3},{3,4},{4,5},{5,6},{6,7},{7,0},{8,9},{9,10},{10,1... | collective-permute-start | bytes 589832 | tf_op jit(solution)/shard_map/ppermute | solution.py:600
  189.7 7.0 %collective-permute-start.28 = (bf16[64,1536]{1,0:T(8,128)(2,1)S(1)}, bf16[64,1536]{1,0:T(8,128)(2,1)S(1)}, u32[]{:S(2)}, u32[]{:S(2)}) collective-permute-start(bf16[64,1536]{1,0:T(8,128)(2,1)S(1)} %collective-permute-done.27.refs_4_), channel_id=1, source_target_pairs={{0,7},{1,0},{2,1},{3,2},{4,3},{5,4},{6,5},{7,6},{8,15},{9,8},{10,9... | collective-permute-start | bytes 589832 | tf_op jit(solution)/shard_map/ppermute | solution.py:601
  193.6 7.3 %collective-permute-start.25 = (bf16[64,1536]{1,0:T(8,128)(2,1)S(1)}, bf16[64,1536]{1,0:T(8,128)(2,1)S(1)}, u32[]{:S(2)}, u32[]{:S(2)}) collective-permute-start(bf16[64,1536]{1,0:T(8,128)(2,1)S(1)} %collective-permute-done.24.refs_1_), channel_id=1, source_target_pairs={{0,1},{1,2},{2,3},{3,4},{4,5},{5,6},{6,7},{7,0},{8,9},{9,10},{10,1... | collective-permute-start | bytes 589832 | tf_op jit(solution)/shard_map/ppermute | solution.py:600
  196.7 7.6 %collective-permute-start.30 = (bf16[32,1536]{1,0:T(8,128)(2,1)S(1)}, bf16[32,1536]{1,0:T(8,128)(2,1)S(1)}, u32[]{:S(2)}, u32[]{:S(2)}) collective-permute-start(bf16[32,1536]{1,0:T(8,128)(2,1)S(1)} %slice.9), channel_id=1, source_target_pairs={{0,7},{1,0},{2,1},{3,2},{4,3},{5,4},{6,5},{7,6},{8,15},{9,8},{10,9... | collective-permute-start | bytes 294920 | tf_op jit(solution)/shard_map/ppermute | solution.py:601
  200.9 4.8 %collective-permute-start.29 = (bf16[32,1536]{1,0:T(8,128)(2,1)S(1)}, bf16[32,1536]{1,0:T(8,128)(2,1)S(1)}, u32[]{:S(2)}, u32[]{:S(2)}) collective-permute-start(bf16[32,1536]{1,0:T(8,128)(2,1)S(1)} %slice.8), channel_id=1, source_target_pairs={{0,1},{1,2},{2,3},{3,4},{4,5},{5,6},{6,7},{7,0},{8,9},{9,10},{10,1... | collective-permute-start | bytes 294920 | tf_op jit(solution)/shard_map/ppermute | solution.py:600
  (46 other events, 218.5 us)
Sparse Core Ops, SparseCore 0:
  112.2 54.1 reduce-scatter.1

commit v3 on v2

--- a/solution.py
+++ b/solution.py
@@ -387,24 +387,26 @@
     )(spot, *operands)
 
 
-def collect_body(mlp_ref, parts_ref, out_ref):
-    height, feat = mlp_ref.shape
-    total = parts_ref[:height, :].astype(f32)
-    for j in range(1, n_col):
-        total = total + parts_ref[j * height : (j + 1) * height, :].astype(f32)
-    out_ref[:, :feat] = mlp_ref[...].astype(bf16)
-    out_ref[:, feat:] = total.astype(bf16)
-
-
-def collect(mlp_sum, parts):
-    height, feat = mlp_sum.shape
+def collect_body(*refs):
+    out_ref = refs[-1]
+    height = out_ref.shape[0]
+    for k, parts_ref in enumerate(refs[:-1]):
+        feat = parts_ref.shape[1]
+        total = parts_ref[:height, :].astype(f32)
+        for j in range(1, n_col):
+            total = total + parts_ref[j * height : (j + 1) * height, :].astype(f32)
+        out_ref[:, k * feat : (k + 1) * feat] = total.astype(bf16)
+
+
+def collect(*parts):
+    rows, feat = parts[0].shape
     return pl.pallas_call(
         collect_body,
-        out_shape=jax.ShapeDtypeStruct((height, 2 * feat), bf16),
+        out_shape=jax.ShapeDtypeStruct((rows // n_col, len(parts) * feat), bf16),
         compiler_params=params(20),
         cost_estimate=cost(1),
         name="collect",
-    )(mlp_sum, parts)
+    )(*parts)
 
 
 def place_body(spot, mine_ref, *refs):
@@ -578,9 +580,7 @@
         grads_near, *tokens_t, *gate_up_far,
     )
     gate_up_near = (right(gate_up_near[0]), left(gate_up_near[1]))
-    mlp_sum = lax.psum_scatter(
-        run(functools.partial(join, f32), mlp_own, mlp_oth), "col", scatter_dimension=0, tiled=True
-    )
+    mlp_parts = trade(run(functools.partial(join, bf16), mlp_own, mlp_oth))
     input_of = lambda block_of, dtype, *weights: run(
         lambda s, g, u, *v: activation_part(input_body, block_of, dtype, "input_part", s, v, [g, u], False),
         spot, *weights, *grads,
@@ -596,7 +596,7 @@
         spot, *tokens_t, grads_last, *gate_up_near,
     )
     gate_up_first, gate_up_second = home_one(first), home_two(second)
-    both = run(collect, mlp_sum, input_parts)
+    both = run(collect, mlp_parts, input_parts)
     col_right = lambda value: lax.ppermute(value, "col", [(i, (i + 1) % n_col) for i in range(n_col)])
     col_left = lambda value: lax.ppermute(value, "col", [(i, (i - 1) % n_col) for i in range(n_col)])
     from_left, from_right = [col_right(both)], [col_left(both)]

time: 215 us -> 207 us (0.963)
  between operations: 14.5 us -> 1.14 us
  starting transfers between devices: 58.5 us -> 63.6 us
    all_to_all x1 -> x2, starting transfers between devices: 8.04 us -> 12.3 us  [local(): trade = lambda value: lax.all_to_all(value, 'col', 0, 0, tiled=True)]
    all_to_all x1 -> x2, waiting for transfers between devices: 0.01 us -> 2.48 us  [local(): trade = lambda value: lax.all_to_all(value, 'col', 0, 0, tiled=True)]
    ppermute x4, starting transfers between devices: 15.2 us -> 12.8 us  [local(): lax.ppermute(value, 'col', [(i, (i - 1) % n_col) for i in range(n_col)])]
    ppermute x2, starting transfers between devices: 8.45 us -> 10.8 us  [local(): home_two = lambda value: lax.ppermute(value, ('depth', 'row'), home_second)]
    unnamed x91 -> x89, local copies, waits for them, and re-layouts: 15.9 us -> 14.7 us
  transfers between devices with their start and end apart: 33 -> 33, of which waited for: 17 -> 17; matrix products, arithmetic and copies ran while one was open for 3% -> 3% of each run, Pallas kernels for 25% -> 27%
where the time goes in v3:
time: 207 us
  starting transfers between devices  63.6 us (31%)
  Pallas kernels  61.7 us (30%)
  waiting for transfers between devices  59.1 us (29%)
  local copies, waits for them, and re-layouts  20.5 us (10%)
    ppermute x4, waiting for transfers between devices, local(): cross = lambda value: lax.ppermute(value, 'row', half_swap)  24.6 us
    unnamed x89, local copies, waits for them, and re-layouts  14.7 us
    pallas_call x4, Pallas kernels, activation_part(): pl.pallas_call(body, grid_spec=pltpu.PrefetchScalarGridSpec(num_scalar_pr...  13.2 us
    ppermute x4, starting transfers between devices, local(): lax.ppermute(value, 'col', [(i, (i - 1) % n_col) for i in range(n_col)])  12.8 us
    all_to_all x2, starting transfers between devices, local(): trade = lambda value: lax.all_to_all(value, 'col', 0, 0, tiled=True)  12.3 us
    pallas_call x2, Pallas kernels, joint_partial(): pl.pallas_call(functools.partial(joint_body, gate_up_step, hg_steps), gri...  11.8 us
    pallas_call x2, Pallas kernels, gate_up_partial(): pl.pallas_call(gate_up_body, grid_spec=pltpu.PrefetchScalarGridSpec(num_s...  11.6 us
    ppermute x7, starting transfers between devices, local(): swap = lambda value: lax.ppermute(value, 'row', core_swap)  11.5 us
  transfers between devices with their start and end apart: 33, of which 17 were waited for; matrix products, arithmetic and copies ran while one was open for 3% of the time, Pallas kernels for 27%

profile of v3, /device:TPU:1, one launch (start us, length us, event | category | flops | bytes accessed | tf_op | source)
XLA Modules:
  0.0 206.6 jit_solution(13788869065232279727)
XLA Ops:
  2.0 3.3 %collective-permute-start = (bf16[512,768]{0,1:T(8,128)(2,1)S(1)}, bf16[512,768]{0,1:T(8,128)(2,1)S(1)}, u32[]{:S(2)}, u32[]{:S(2)}) collective-permute-start(bf16[512,768]{0,1:T(8,128)(2,1)S(1)} %copy.10), channel_id=1, source_target_pairs={{0,8},{8,0},{16,24},{24,16},{1,9},{9,1},{17,25},{25,17},{2,10},{10... | collective-permute-start | bytes 2359304 | tf_op jit(solution)/shard_map/ppermute | solution.py:495
  13.1 4.4 %gate_up_partial.2 = (f32[512,512]{1,0:T(8,128)}, bf16[512,512]{1,0:T(8,128)(2,1)}) custom-call(s32[4]{0:T(128)} %pad_add_fusion.spot, bf16[512,768]{1,0:T(8,128)(2,1)} %refs_0_.2, bf16[512,768]{1,0:T(8,128)(2,1)} %copy.11.oth_ref.refs_1_, bf16[768,2048]{1,0:T(8,128)(2,1)} %g0.1, bf16[768,2048]{1,0:T(8,128)(2,1)} %u0.1, ...), custom_call_target="tpu_custom_call" | custom-call | flops 1 | bytes 14850000 | tf_op jit(solution)/shard_map/gate_up_partial/pallas_call | solution.py:98
  20.5 7.2 %gate_up_partial.3 = (f32[512,1024]{1,0:T(8,128)}, bf16[512,1024]{1,0:T(8,128)(2,1)}) custom-call(s32[4]{0:T(128)} %pad_add_fusion.spot, bf16[512,768]{1,0:T(8,128)(2,1)} %refs_0_.2, bf16[512,768]{1,0:T(8,128)(2,1)} %copy.11.oth_ref.refs_1_, bf16[768,2048]{1,0:T(8,128)(2,1)} %g0.1, bf16[768,2048]{1,0:T(8,128)(2,1)} %u0.1, ...), custom_call_target="tpu_custom_call" | custom-call | flops 1 | bytes 14850000 | tf_op jit(solution)/shard_map/gate_up_partial/pallas_call | solution.py:98
  27.8 4.9 %collective-permute-done.3.got_ref = bf16[512,512]{1,0:T(8,128)(2,1)S(1)} collective-permute-done((bf16[512,512]{1,0:T(8,128)(2,1)}, bf16[512,512]{1,0:T(8,128)(2,1)S(1)}, u32[]{:S(2)}, u32[]{:S(2)}) %collective-permute-start.3) | collective-permute-done | bytes 524320 | tf_op jit(solution)/shard_map/ppermute | solution.py:496
  35.4 2.6 %collective-permute-start.8 = (bf16[256,768]{1,0:T(8,128)(2,1)S(1)}, bf16[256,768]{1,0:T(8,128)(2,1)S(1)}, u32[]{:S(2)}, u32[]{:S(2)}) collective-permute-start(bf16[256,768]{1,0:T(8,128)(2,1)S(1)} %get-tuple-element.92), channel_id=1, source_target_pairs={{0,96},{32,0},{64,32},{96,64},{128,224},{160,128},{192,160},{224,1... | collective-permute-start | bytes 1179656 | tf_op jit(solution)/shard_map/ppermute | solution.py:498
  39.1 6.2 %joint_partial.2 = (f32[512,512]{1,0:T(8,128)}, f32[512,256]{1,0:T(8,128)}, bf16[512,768]{1,0:T(8,128)(2,1)}) custom-call(s32[4]{0:T(128)} %pad_add_fusion.spot, bf16[512,768]{1,0:T(8,128)(2,1)} %refs_0_.2, bf16[512,768]{1,0:T(8,128)(2,1)} %copy.11.oth_ref.refs_1_, bf16[768,2048]{1,0:T(8,128)(2,1)} %g0.1, bf16[768,2048]{1,0:T(8,128)(2,1)} %u0.1, ...), custom_call_target="tpu_custom_call" | custom-call | flops 1 | bytes 19800000 | tf_op jit(solution)/shard_map/joint_partial/pallas_call | solution.py:156
  45.3 12.8 %collective-permute-done.6.got_ref = bf16[512,1024]{1,0:T(8,128)(2,1)S(1)} collective-permute-done((bf16[512,1024]{1,0:T(8,128)(2,1)}, bf16[512,1024]{1,0:T(8,128)(2,1)S(1)}, u32[]{:S(2)}, u32[]{:S(2)}) %collective-permute-start.6) | collective-permute-done | bytes 1048608 | tf_op jit(solution)/shard_map/ppermute | solution.py:496
  65.3 5.7 %joint_partial.3 = (f32[512,768]{1,0:T(8,128)}, bf16[512,768]{1,0:T(8,128)(2,1)}) custom-call(s32[4]{0:T(128)} %pad_add_fusion.spot, bf16[512,768]{1,0:T(8,128)(2,1)} %b0.5, bf16[512,768]{1,0:T(8,128)(2,1)} %copy-done.10, bf16[2048,768]{1,0:T(8,128)(2,1)} %w0.1, bf16[1024,768]{1,0:T(8,128)(2,1)} %copy-done.5, bf16[2048,768]{1,0:T(8,128)(2,1)} %w0.1, ...), custom_call_target="tpu_custom_call" | custom-call | flops 1 | bytes 19800000 | tf_op jit(solution)/shard_map/joint_partial/pallas_call | solution.py:156
  71.3 5.7 %collective-permute-done.9.hg_got_ref.got_ref = bf16[512,768]{1,0:T(8,128)(2,1)S(1)} collective-permute-done((bf16[512,768]{1,0:T(8,128)(2,1)}, bf16[512,768]{1,0:T(8,128)(2,1)S(1)}, u32[]{:S(2)}, u32[]{:S(2)}) %collective-permute-start.9) | collective-permute-done | bytes 786464 | tf_op jit(solution)/shard_map/ppermute | solution.py:496
  86.0 2.7 %last_terms.2 = (f32[256,768]{1,0:T(8,128)S(1)}, bf16[256,768]{1,0:T(8,128)(2,1)S(1)}, bf16[256,768]{1,0:T(8,128)(2,1)S(1)}) custom-call(s32[4]{0:T(128)S(1)} %copy-done.40, bf16[256,512]{1,0:T(8,128)(2,1)S(1)} %get-tuple-element.107.a0.a1, bf16[256,512]{1,0:T(8,128)(2,1)S(1)} %get-tuple-element.107.a0.a1, bf16[512,768]{1,0:T(8,128)(2,1)S(1)} %copy-done.9, ...), custom_call_target="tpu_custom_call" | custom-call | flops 1 | bytes 4290000 | tf_op jit(solution)/shard_map/last_terms/pallas_call | solution.py:371
  92.6 3.6 %collective-permute-start.15 = (bf16[512,768]{1,0:T(8,128)(2,1)S(1)}, bf16[512,768]{1,0:T(8,128)(2,1)S(1)}, u32[]{:S(2)}, u32[]{:S(2)}) collective-permute-start(bf16[512,768]{1,0:T(8,128)(2,1)S(1)} %mlp_part.2), channel_id=1, source_target_pairs={{0,8},{8,0},{16,24},{24,16},{1,9},{9,1},{17,25},{25,17},{2,10},{10... | collective-permute-start | bytes 2359304 | tf_op jit(solution)/shard_map/ppermute | solution.py:495
  101.0 3.0 %near_terms.3 = (bf16[1536,512]{1,0:T(8,128)(2,1)}, bf16[1536,512]{1,0:T(8,128)(2,1)}) custom-call(bf16[768,512]{1,0:T(8,128)(2,1)S(1)} %bitcast.15, bf16[768,512]{1,0:T(8,128)(2,1)S(1)} %bitcast.11, bf16[768,512]{1,0:T(8,128)(2,1)S(1)} %bitcast.16, bf16[768,512]{1,0:T(8,128)(2,1)S(1)} %bitcast.12, bf16[512,1024]{1,0:T(8,128)(2,1)S(1)} %grads_step.4.b0.b1.d0.d1.near_ref, ...), custom_call_target="tpu_custom_call" | custom-call | flops 1 | bytes 7260000 | tf_op jit(solution)/shard_map/near_terms/pallas_call | solution.py:340
  105.1 7.9 %all-to-all-start = ((bf16[8,64,768]{2,1,0:T(8,128)(2,1)}), bf16[8,64,768]{2,1,0:T(8,128)(2,1)}, u32[]{:S(2)}, u32[]{:S(2)}) async-start(bf16[8,64,768]{2,1,0:T(8,128)(2,1)} %bitcast.20), calls=%async_computation | async-start | bytes 1572864 | tf_op jit(solution)/shard_map/all_to_all | solution.py:501
  114.0 5.1 %input_part.2 = bf16[512,768]{1,0:T(8,128)(2,1)S(1)} custom-call(s32[4]{0:T(128)S(1)} %copy-done.40, bf16[512,512]{1,0:T(8,128)(2,1)S(1)} %copy-done.16, bf16[512,1024]{1,0:T(8,128)(2,1)S(1)} %grads_step.4.b0.b1.d0.d1.near_ref, bf16[512,512]{1,0:T(8,128)(2,1)S(1)} %grads_step.5.last_ref.b0.b1, ...), custom_call_target="tpu_custom_call" | custom-call | flops 1 | bytes 8250000 | tf_op jit(solution)/shard_map/input_part/pallas_call | solution.py:262
  119.1 3.9 %collective-permute-start.16 = (bf16[512,768]{1,0:T(8,128)(2,1)S(1)}, bf16[512,768]{1,0:T(8,128)(2,1)S(1)}, u32[]{:S(2)}, u32[]{:S(2)}) collective-permute-start(bf16[512,768]{1,0:T(8,128)(2,1)S(1)} %input_part.2), channel_id=1, source_target_pairs={{0,8},{8,0},{16,24},{24,16},{1,9},{9,1},{17,25},{25,17},{2,10},{10... | collective-permute-start | bytes 2359304 | tf_op jit(solution)/shard_map/ppermute | solution.py:495
  123.0 2.8 %collective-permute-start.20 = (bf16[1536,512]{1,0:T(8,128)(2,1)}, bf16[1536,512]{1,0:T(8,128)(2,1)}, u32[]{:S(2)}, u32[]{:S(2)}) collective-permute-start(bf16[1536,512]{1,0:T(8,128)(2,1)} %get-tuple-element.126), channel_id=1, source_target_pairs={{0,96},{32,0},{64,32},{96,64},{128,224},{160,128},{192,160},{224,1... | collective-permute-start | bytes 4718600 | tf_op jit(solution)/shard_map/ppermute | solution.py:498
  125.8 3.6 %input_part.3.own_ref = f32[512,768]{1,0:T(8,128)S(1)} custom-call(s32[4]{0:T(128)S(1)} %copy-done.40, bf16[512,512]{1,0:T(8,128)(2,1)S(1)} %copy-done.16, bf16[512,1024]{1,0:T(8,128)(2,1)S(1)} %grads_step.4.b0.b1.d0.d1.near_ref, bf16[512,512]{1,0:T(8,128)(2,1)S(1)} %grads_step.5.last_ref.b0.b1, bf16[768,2048]{1,0:T(8,128)(2,1)S(1)} %copy-done.2, ...), custom_call_target="tpu_custom_call" | custom-call | flops 1 | bytes 8250000 | tf_op jit(solution)/shard_map/input_part/pallas_call | solution.py:262
  133.0 4.5 %all-to-all-start.1 = ((bf16[8,64,768]{2,1,0:T(8,128)(2,1)}), bf16[8,64,768]{2,1,0:T(8,128)(2,1)S(1)}, u32[]{:S(2)}, u32[]{:S(2)}) async-start(bf16[8,64,768]{2,1,0:T(8,128)(2,1)} %bitcast.19), calls=%async_computation.1 | async-start | bytes 1572864 | tf_op jit(solution)/shard_map/all_to_all | solution.py:501
  137.9 6.4 %collective-permute-start.18 = (bf16[256,768]{1,0:T(8,128)(2,1)S(1)}, bf16[256,768]{1,0:T(8,128)(2,1)S(1)}, u32[]{:S(2)}, u32[]{:S(2)}) collective-permute-start(bf16[256,768]{1,0:T(8,128)(2,1)S(1)} %get-tuple-element.124), channel_id=1, source_target_pairs={{8,128},{24,144},{40,160},{56,176},{72,192},{88,208},{104,224},{12... | collective-permute-start | bytes 1179656 | tf_op jit(solution)/shard_map/ppermute | solution.py:500
  144.3 8.4 %collective-permute-done.18.two_ref = bf16[256,768]{1,0:T(8,128)(2,1)S(1)} collective-permute-done((bf16[256,768]{1,0:T(8,128)(2,1)S(1)}, bf16[256,768]{1,0:T(8,128)(2,1)S(1)}, u32[]{:S(2)}, u32[]{:S(2)}) %collective-permute-start.18) | collective-permute-done | bytes 393248 | tf_op jit(solution)/shard_map/ppermute | solution.py:500
  155.4 4.5 %collective-permute-done.20.from_right = bf16[1536,512]{1,0:T(8,128)(2,1)} collective-permute-done((bf16[1536,512]{1,0:T(8,128)(2,1)}, bf16[1536,512]{1,0:T(8,128)(2,1)}, u32[]{:S(2)}, u32[]{:S(2)}) %collective-permute-start.20) | collective-permute-done | bytes 1572896 | tf_op jit(solution)/shard_map/ppermute | solution.py:498
  159.9 3.1 %collective-permute-done.19.from_left = bf16[1536,512]{1,0:T(8,128)(2,1)} collective-permute-done((bf16[1536,512]{1,0:T(8,128)(2,1)}, bf16[1536,512]{1,0:T(8,128)(2,1)}, u32[]{:S(2)}, u32[]{:S(2)}) %collective-permute-start.19) | collective-permute-done | bytes 1572896 | tf_op jit(solution)/shard_map/ppermute | solution.py:497
  163.0 4.7 %last_terms.3 = (f32[768,512]{1,0:T(8,128)S(1)}, bf16[768,512]{1,0:T(8,128)(2,1)}, bf16[768,512]{1,0:T(8,128)(2,1)}) custom-call(s32[4]{0:T(128)S(1)} %copy-done.40, bf16[768,512]{1,0:T(8,128)(2,1)S(1)} %bitcast.17, bf16[768,512]{1,0:T(8,128)(2,1)S(1)} %bitcast.13, bf16[512,512]{1,0:T(8,128)(2,1)S(1)} %grads_step.5.last_ref.b0.b1, ...), custom_call_target="tpu_custom_call" | custom-call | flops 1 | bytes 4290000 | tf_op jit(solution)/shard_map/last_terms/pallas_call | solution.py:371
  169.1 4.4 %collective-permute-start.22 = (bf16[768,512]{1,0:T(8,128)(2,1)}, bf16[768,512]{1,0:T(8,128)(2,1)}, u32[]{:S(2)}, u32[]{:S(2)}) collective-permute-start(bf16[768,512]{1,0:T(8,128)(2,1)} %get-tuple-element.131), channel_id=1, source_target_pairs={{8,128},{24,144},{40,160},{56,176},{72,192},{88,208},{104,224},{12... | collective-permute-start | bytes 2359304 | tf_op jit(solution)/shard_map/ppermute | solution.py:500
  174.9 3.0 %collective-permute-start.26 = (bf16[64,1536]{1,0:T(8,128)(2,1)S(1)}, bf16[64,1536]{1,0:T(8,128)(2,1)S(1)}, u32[]{:S(2)}, u32[]{:S(2)}) collective-permute-start(bf16[64,1536]{1,0:T(8,128)(2,1)S(1)} %collect.1.mine_ref), channel_id=1, source_target_pairs={{0,7},{1,0},{2,1},{3,2},{4,3},{5,4},{6,5},{7,6},{8,15},{9,8},{10,9... | collective-permute-start | bytes 589832 | tf_op jit(solution)/shard_map/ppermute | solution.py:601
  177.9 3.3 %collective-permute-done.26.refs_3_ = bf16[64,1536]{1,0:T(8,128)(2,1)S(1)} collective-permute-done((bf16[64,1536]{1,0:T(8,128)(2,1)S(1)}, bf16[64,1536]{1,0:T(8,128)(2,1)S(1)}, u32[]{:S(2)}, u32[]{:S(2)}) %collective-permute-start.26) | collective-permute-done | bytes 196640 | tf_op jit(solution)/shard_map/ppermute | solution.py:601
  181.2 3.1 %collective-permute-start.27 = (bf16[64,1536]{1,0:T(8,128)(2,1)S(1)}, bf16[64,1536]{1,0:T(8,128)(2,1)S(1)}, u32[]{:S(2)}, u32[]{:S(2)}) collective-permute-start(bf16[64,1536]{1,0:T(8,128)(2,1)S(1)} %collective-permute-done.26.refs_3_), channel_id=1, source_target_pairs={{0,7},{1,0},{2,1},{3,2},{4,3},{5,4},{6,5},{7,6},{8,15},{9,8},{10,9... | collective-permute-start | bytes 589832 | tf_op jit(solution)/shard_map/ppermute | solution.py:601
  184.6 4.1 %collective-permute-done.27.refs_4_ = bf16[64,1536]{1,0:T(8,128)(2,1)S(1)} collective-permute-done((bf16[64,1536]{1,0:T(8,128)(2,1)S(1)}, bf16[64,1536]{1,0:T(8,128)(2,1)S(1)}, u32[]{:S(2)}, u32[]{:S(2)}) %collective-permute-start.27) | collective-permute-done | bytes 196640 | tf_op jit(solution)/shard_map/ppermute | solution.py:601
  188.7 3.1 %collective-permute-start.28 = (bf16[64,1536]{1,0:T(8,128)(2,1)S(1)}, bf16[64,1536]{1,0:T(8,128)(2,1)S(1)}, u32[]{:S(2)}, u32[]{:S(2)}) collective-permute-start(bf16[64,1536]{1,0:T(8,128)(2,1)S(1)} %collective-permute-done.27.refs_4_), channel_id=1, source_target_pairs={{0,7},{1,0},{2,1},{3,2},{4,3},{5,4},{6,5},{7,6},{8,15},{9,8},{10,9... | collective-permute-start | bytes 589832 | tf_op jit(solution)/shard_map/ppermute | solution.py:601
  192.7 3.1 %collective-permute-done.28.refs_5_ = bf16[64,1536]{1,0:T(8,128)(2,1)S(1)} collective-permute-done((bf16[64,1536]{1,0:T(8,128)(2,1)S(1)}, bf16[64,1536]{1,0:T(8,128)(2,1)S(1)}, u32[]{:S(2)}, u32[]{:S(2)}) %collective-permute-start.28) | collective-permute-done | bytes 196640 | tf_op jit(solution)/shard_map/ppermute | solution.py:601
  195.8 3.5 %collective-permute-start.30 = (bf16[32,1536]{1,0:T(8,128)(2,1)S(1)}, bf16[32,1536]{1,0:T(8,128)(2,1)S(1)}, u32[]{:S(2)}, u32[]{:S(2)}) collective-permute-start(bf16[32,1536]{1,0:T(8,128)(2,1)S(1)} %slice.9), channel_id=1, source_target_pairs={{0,7},{1,0},{2,1},{3,2},{4,3},{5,4},{6,5},{7,6},{8,15},{9,8},{10,9... | collective-permute-start | bytes 294920 | tf_op jit(solution)/shard_map/ppermute | solution.py:601
  200.2 3.3 %finish.3 = (f32[1,768,256]{2,1,0:T(8,128)}, f32[1,768,256]{2,1,0:T(8,128)}) custom-call(s32[4]{0:T(128)S(1)} %copy-done.40, bf16[768,512]{1,0:T(8,128)(2,1)} %collective-permute-done.21.one_ref, f32[768,512]{1,0:T(8,128)S(1)} %copy-done.34, bf16[768,512]{1,0:T(8,128)(2,1)} %collective-permute-done.22.two_ref), custom_call_target="tpu_custom_call" | custom-call | flops 1 | bytes 4950000 | tf_op jit(solution)/shard_map/finish/pallas_call | solution.py:470
  (157 shorter events, 57.7 us)
Async XLA Ops:
  2.0 5.2 %collective-permute-start = (bf16[512,768]{0,1:T(8,128)(2,1)S(1)}, bf16[512,768]{0,1:T(8,128)(2,1)S(1)}, u32[]{:S(2)}, u32[]{:S(2)}) collective-permute-start(bf16[512,768]{0,1:T(8,128)(2,1)S(1)} %copy.10), channel_id=1, source_target_pairs={{0,8},{8,0},{16,24},{24,16},{1,9},{9,1},{17,25},{25,17},{2,10},{10... | collective-permute-start | bytes 2359304 | tf_op jit(solution)/shard_map/ppermute | solution.py:495
  9.1 4.0 %collective-permute-start.2 = (bf16[768,1024]{1,0:T(8,128)(2,1)}, bf16[768,1024]{1,0:T(8,128)(2,1)}, u32[]{:S(2)}, u32[]{:S(2)}) collective-permute-start(bf16[768,1024]{1,0:T(8,128)(2,1)} %constant_dynamic-slice_fusion.1), channel_id=1, source_target_pairs={{0,8},{8,0},{16,24},{24,16},{1,9},{9,1},{17,25},{25,17},{2,10},{10... | collective-permute-start | bytes 4718600 | tf_op jit(solution)/shard_map/ppermute | solution.py:495
  17.5 15.2 %collective-permute-start.3 = (bf16[512,512]{1,0:T(8,128)(2,1)}, bf16[512,512]{1,0:T(8,128)(2,1)S(1)}, u32[]{:S(2)}, u32[]{:S(2)}) collective-permute-start(bf16[512,512]{1,0:T(8,128)(2,1)} %get-tuple-element.79), channel_id=1, source_target_pairs={{0,16},{16,0},{8,24},{24,8},{1,17},{17,1},{9,25},{25,9},{2,18},{18... | collective-permute-start | bytes 1572872 | tf_op jit(solution)/shard_map/ppermute | solution.py:496
  20.0 17.9 %collective-permute-start.5 = (bf16[1024,768]{1,0:T(8,128)(2,1)}, bf16[1024,768]{1,0:T(8,128)(2,1)S(1)}, u32[]{:S(2)}, u32[]{:S(2)}) collective-permute-start(bf16[1024,768]{1,0:T(8,128)(2,1)} %constant_dynamic-slice_fusion), channel_id=1, source_target_pairs={{0,8},{8,0},{16,24},{24,16},{1,9},{9,1},{17,25},{25,17},{2,10},{10... | collective-permute-start | bytes 4718600 | tf_op jit(solution)/shard_map/ppermute | solution.py:495
  20.5 14.3 %collective-permute-start.4 = (bf16[512,768]{1,0:T(8,128)(2,1)S(1)}, bf16[512,768]{1,0:T(8,128)(2,1)S(1)}, u32[]{:S(2)}, u32[]{:S(2)}) collective-permute-start(bf16[512,768]{1,0:T(8,128)(2,1)S(1)} %copy-done.7), channel_id=1, source_target_pairs={{0,8},{8,0},{16,24},{24,16},{1,9},{9,1},{17,25},{25,17},{2,10},{10... | collective-permute-start | bytes 2359304 | tf_op jit(solution)/shard_map/ppermute | solution.py:495
  32.7 25.4 %collective-permute-start.6 = (bf16[512,1024]{1,0:T(8,128)(2,1)}, bf16[512,1024]{1,0:T(8,128)(2,1)S(1)}, u32[]{:S(2)}, u32[]{:S(2)}) collective-permute-start(bf16[512,1024]{1,0:T(8,128)(2,1)} %get-tuple-element.88), channel_id=1, source_target_pairs={{0,16},{16,0},{8,24},{24,8},{1,17},{17,1},{9,25},{25,9},{2,18},{18... | collective-permute-start | bytes 3145736 | tf_op jit(solution)/shard_map/ppermute | solution.py:496
  35.4 25.5 %collective-permute-start.8 = (bf16[256,768]{1,0:T(8,128)(2,1)S(1)}, bf16[256,768]{1,0:T(8,128)(2,1)S(1)}, u32[]{:S(2)}, u32[]{:S(2)}) collective-permute-start(bf16[256,768]{1,0:T(8,128)(2,1)S(1)} %get-tuple-element.92), channel_id=1, source_target_pairs={{0,96},{32,0},{64,32},{96,64},{128,224},{160,128},{192,160},{224,1... | collective-permute-start | bytes 1179656 | tf_op jit(solution)/shard_map/ppermute | solution.py:498
  37.9 22.9 %collective-permute-start.7 = (bf16[256,768]{1,0:T(8,128)(2,1)S(1)}, bf16[256,768]{1,0:T(8,128)(2,1)S(1)}, u32[]{:S(2)}, u32[]{:S(2)}) collective-permute-start(bf16[256,768]{1,0:T(8,128)(2,1)S(1)} %get-tuple-element.83), channel_id=1, source_target_pairs={{0,32},{32,64},{64,96},{96,0},{128,160},{160,192},{192,224},{224,1... | collective-permute-start | bytes 1179656 | tf_op jit(solution)/shard_map/ppermute | solution.py:497
  58.1 18.9 %collective-permute-start.9 = (bf16[512,768]{1,0:T(8,128)(2,1)}, bf16[512,768]{1,0:T(8,128)(2,1)S(1)}, u32[]{:S(2)}, u32[]{:S(2)}) collective-permute-start(bf16[512,768]{1,0:T(8,128)(2,1)} %get-tuple-element.101), channel_id=1, source_target_pairs={{0,16},{16,0},{8,24},{24,8},{1,17},{17,1},{9,25},{25,9},{2,18},{18... | collective-permute-start | bytes 2359304 | tf_op jit(solution)/shard_map/ppermute | solution.py:496
  62.8 23.1 %collective-permute-start.11 = (bf16[512,768]{1,0:T(8,128)(2,1)}, bf16[512,768]{1,0:T(8,128)(2,1)}, u32[]{:S(2)}, u32[]{:S(2)}) collective-permute-start(bf16[512,768]{1,0:T(8,128)(2,1)} %get-tuple-element.108), channel_id=1, source_target_pairs={{0,96},{32,0},{64,32},{96,64},{128,224},{160,128},{192,160},{224,1... | collective-permute-start | bytes 2359304 | tf_op jit(solution)/shard_map/ppermute | solution.py:498
  65.3 20.6 %collective-permute-start.10 = (bf16[512,768]{1,0:T(8,128)(2,1)}, bf16[512,768]{1,0:T(8,128)(2,1)}, u32[]{:S(2)}, u32[]{:S(2)}) collective-permute-start(bf16[512,768]{1,0:T(8,128)(2,1)} %get-tuple-element.93), channel_id=1, source_target_pairs={{0,32},{32,64},{64,96},{96,0},{128,160},{160,192},{192,224},{224,1... | collective-permute-start | bytes 2359304 | tf_op jit(solution)/shard_map/ppermute | solution.py:497
  81.5 19.5 %collective-permute-start.13 = (bf16[768,512]{1,0:T(8,128)(2,1)S(1)}, bf16[768,512]{1,0:T(8,128)(2,1)S(1)}, u32[]{:S(2)}, u32[]{:S(2)}) collective-permute-start(bf16[768,512]{1,0:T(8,128)(2,1)S(1)} %get-tuple-element.103), channel_id=1, source_target_pairs={{0,32},{32,64},{64,96},{96,0},{128,160},{160,192},{192,224},{224,1... | collective-permute-start | bytes 2359304 | tf_op jit(solution)/shard_map/ppermute | solution.py:497
  81.8 17.8 %collective-permute-start.12 = (bf16[512,768]{1,0:T(8,128)(2,1)S(1)}, bf16[512,768]{1,0:T(8,128)(2,1)S(1)}, u32[]{:S(2)}, u32[]{:S(2)}) collective-permute-start(bf16[512,768]{1,0:T(8,128)(2,1)S(1)} %copy-done.43), channel_id=1, source_target_pairs={{0,16},{16,0},{8,24},{24,8},{1,17},{17,1},{9,25},{25,9},{2,18},{18... | collective-permute-start | bytes 2359304 | tf_op jit(solution)/shard_map/ppermute | solution.py:496
  84.2 16.8 %collective-permute-start.14 = (bf16[768,512]{1,0:T(8,128)(2,1)S(1)}, bf16[768,512]{1,0:T(8,128)(2,1)S(1)}, u32[]{:S(2)}, u32[]{:S(2)}) collective-permute-start(bf16[768,512]{1,0:T(8,128)(2,1)S(1)} %get-tuple-element.117), channel_id=1, source_target_pairs={{0,96},{32,0},{64,32},{96,64},{128,224},{160,128},{192,160},{224,1... | collective-permute-start | bytes 2359304 | tf_op jit(solution)/shard_map/ppermute | solution.py:498
  92.6 11.5 %collective-permute-start.15 = (bf16[512,768]{1,0:T(8,128)(2,1)S(1)}, bf16[512,768]{1,0:T(8,128)(2,1)S(1)}, u32[]{:S(2)}, u32[]{:S(2)}) collective-permute-start(bf16[512,768]{1,0:T(8,128)(2,1)S(1)} %mlp_part.2), channel_id=1, source_target_pairs={{0,8},{8,0},{16,24},{24,16},{1,9},{9,1},{17,25},{25,17},{2,10},{10... | collective-permute-start | bytes 2359304 | tf_op jit(solution)/shard_map/ppermute | solution.py:495
  105.1 28.0 %all-to-all-start = ((bf16[8,64,768]{2,1,0:T(8,128)(2,1)}), bf16[8,64,768]{2,1,0:T(8,128)(2,1)}, u32[]{:S(2)}, u32[]{:S(2)}) async-start(bf16[8,64,768]{2,1,0:T(8,128)(2,1)} %bitcast.20), calls=%async_computation | async-start | bytes 1572864 | tf_op jit(solution)/shard_map/all_to_all | solution.py:501
  119.1 10.4 %collective-permute-start.16 = (bf16[512,768]{1,0:T(8,128)(2,1)S(1)}, bf16[512,768]{1,0:T(8,128)(2,1)S(1)}, u32[]{:S(2)}, u32[]{:S(2)}) collective-permute-start(bf16[512,768]{1,0:T(8,128)(2,1)S(1)} %input_part.2), channel_id=1, source_target_pairs={{0,8},{8,0},{16,24},{24,16},{1,9},{9,1},{17,25},{25,17},{2,10},{10... | collective-permute-start | bytes 2359304 | tf_op jit(solution)/shard_map/ppermute | solution.py:495
  123.0 36.9 %collective-permute-start.20 = (bf16[1536,512]{1,0:T(8,128)(2,1)}, bf16[1536,512]{1,0:T(8,128)(2,1)}, u32[]{:S(2)}, u32[]{:S(2)}) collective-permute-start(bf16[1536,512]{1,0:T(8,128)(2,1)} %get-tuple-element.126), channel_id=1, source_target_pairs={{0,96},{32,0},{64,32},{96,64},{128,224},{160,128},{192,160},{224,1... | collective-permute-start | bytes 4718600 | tf_op jit(solution)/shard_map/ppermute | solution.py:498
  125.8 37.2 %collective-permute-start.19 = (bf16[1536,512]{1,0:T(8,128)(2,1)}, bf16[1536,512]{1,0:T(8,128)(2,1)}, u32[]{:S(2)}, u32[]{:S(2)}) collective-permute-start(bf16[1536,512]{1,0:T(8,128)(2,1)} %get-tuple-element.118), channel_id=1, source_target_pairs={{0,32},{32,64},{64,96},{96,0},{128,160},{160,192},{192,224},{224,1... | collective-permute-start | bytes 4718600 | tf_op jit(solution)/shard_map/ppermute | solution.py:497
  133.0 40.5 %all-to-all-start.1 = ((bf16[8,64,768]{2,1,0:T(8,128)(2,1)}), bf16[8,64,768]{2,1,0:T(8,128)(2,1)S(1)}, u32[]{:S(2)}, u32[]{:S(2)}) async-start(bf16[8,64,768]{2,1,0:T(8,128)(2,1)} %bitcast.19), calls=%async_computation.1 | async-start | bytes 1572864 | tf_op jit(solution)/shard_map/all_to_all | solution.py:501
  137.5 6.8 %collective-permute-start.17 = (bf16[256,768]{1,0:T(8,128)(2,1)}, bf16[256,768]{1,0:T(8,128)(2,1)S(1)}, u32[]{:S(2)}, u32[]{:S(2)}) collective-permute-start(bf16[256,768]{1,0:T(8,128)(2,1)} %copy-done.41), channel_id=1, source_target_pairs={{0,8},{8,136},{16,24},{24,152},{32,40},{40,168},{48,56},{56,184},{... | collective-permute-start | bytes 1179656 | tf_op jit(solution)/shard_map/ppermute | solution.py:499
  137.9 14.7 %collective-permute-start.18 = (bf16[256,768]{1,0:T(8,128)(2,1)S(1)}, bf16[256,768]{1,0:T(8,128)(2,1)S(1)}, u32[]{:S(2)}, u32[]{:S(2)}) collective-permute-start(bf16[256,768]{1,0:T(8,128)(2,1)S(1)} %get-tuple-element.124), channel_id=1, source_target_pairs={{8,128},{24,144},{40,160},{56,176},{72,192},{88,208},{104,224},{12... | collective-permute-start | bytes 1179656 | tf_op jit(solution)/shard_map/ppermute | solution.py:500
  168.9 31.3 %collective-permute-start.21 = (bf16[768,512]{1,0:T(8,128)(2,1)}, bf16[768,512]{1,0:T(8,128)(2,1)}, u32[]{:S(2)}, u32[]{:S(2)}) collective-permute-start(bf16[768,512]{1,0:T(8,128)(2,1)} %get-tuple-element.130), channel_id=1, source_target_pairs={{0,8},{8,136},{16,24},{24,152},{32,40},{40,168},{48,56},{56,184},{... | collective-permute-start | bytes 2359304 | tf_op jit(solution)/shard_map/ppermute | solution.py:499
  169.1 31.0 %collective-permute-start.22 = (bf16[768,512]{1,0:T(8,128)(2,1)}, bf16[768,512]{1,0:T(8,128)(2,1)}, u32[]{:S(2)}, u32[]{:S(2)}) collective-permute-start(bf16[768,512]{1,0:T(8,128)(2,1)} %get-tuple-element.131), channel_id=1, source_target_pairs={{8,128},{24,144},{40,160},{56,176},{72,192},{88,208},{104,224},{12... | collective-permute-start | bytes 2359304 | tf_op jit(solution)/shard_map/ppermute | solution.py:500
  174.9 6.3 %collective-permute-start.26 = (bf16[64,1536]{1,0:T(8,128)(2,1)S(1)}, bf16[64,1536]{1,0:T(8,128)(2,1)S(1)}, u32[]{:S(2)}, u32[]{:S(2)}) collective-permute-start(bf16[64,1536]{1,0:T(8,128)(2,1)S(1)} %collect.1.mine_ref), channel_id=1, source_target_pairs={{0,7},{1,0},{2,1},{3,2},{4,3},{5,4},{6,5},{7,6},{8,15},{9,8},{10,9... | collective-permute-start | bytes 589832 | tf_op jit(solution)/shard_map/ppermute | solution.py:601
  177.9 6.7 %collective-permute-start.23 = (bf16[64,1536]{1,0:T(8,128)(2,1)S(1)}, bf16[64,1536]{1,0:T(8,128)(2,1)S(1)}, u32[]{:S(2)}, u32[]{:S(2)}) collective-permute-start(bf16[64,1536]{1,0:T(8,128)(2,1)S(1)} %collect.1.mine_ref), channel_id=1, source_target_pairs={{0,1},{1,2},{2,3},{3,4},{4,5},{5,6},{6,7},{7,0},{8,9},{9,10},{10,1... | collective-permute-start | bytes 589832 | tf_op jit(solution)/shard_map/ppermute | solution.py:600
  181.2 7.5 %collective-permute-start.27 = (bf16[64,1536]{1,0:T(8,128)(2,1)S(1)}, bf16[64,1536]{1,0:T(8,128)(2,1)S(1)}, u32[]{:S(2)}, u32[]{:S(2)}) collective-permute-start(bf16[64,1536]{1,0:T(8,128)(2,1)S(1)} %collective-permute-done.26.refs_3_), channel_id=1, source_target_pairs={{0,7},{1,0},{2,1},{3,2},{4,3},{5,4},{6,5},{7,6},{8,15},{9,8},{10,9... | collective-permute-start | bytes 589832 | tf_op jit(solution)/shard_map/ppermute | solution.py:601
  184.6 8.1 %collective-permute-start.24 = (bf16[64,1536]{1,0:T(8,128)(2,1)S(1)}, bf16[64,1536]{1,0:T(8,128)(2,1)S(1)}, u32[]{:S(2)}, u32[]{:S(2)}) collective-permute-start(bf16[64,1536]{1,0:T(8,128)(2,1)S(1)} %collective-permute-done.23.refs_0_), channel_id=1, source_target_pairs={{0,1},{1,2},{2,3},{3,4},{4,5},{5,6},{6,7},{7,0},{8,9},{9,10},{10,1... | collective-permute-start | bytes 589832 | tf_op jit(solution)/shard_map/ppermute | solution.py:600
  188.7 7.0 %collective-permute-start.28 = (bf16[64,1536]{1,0:T(8,128)(2,1)S(1)}, bf16[64,1536]{1,0:T(8,128)(2,1)S(1)}, u32[]{:S(2)}, u32[]{:S(2)}) collective-permute-start(bf16[64,1536]{1,0:T(8,128)(2,1)S(1)} %collective-permute-done.27.refs_4_), channel_id=1, source_target_pairs={{0,7},{1,0},{2,1},{3,2},{4,3},{5,4},{6,5},{7,6},{8,15},{9,8},{10,9... | collective-permute-start | bytes 589832 | tf_op jit(solution)/shard_map/ppermute | solution.py:601
  192.7 7.3 %collective-permute-start.25 = (bf16[64,1536]{1,0:T(8,128)(2,1)S(1)}, bf16[64,1536]{1,0:T(8,128)(2,1)S(1)}, u32[]{:S(2)}, u32[]{:S(2)}) collective-permute-start(bf16[64,1536]{1,0:T(8,128)(2,1)S(1)} %collective-permute-done.24.refs_1_), channel_id=1, source_target_pairs={{0,1},{1,2},{2,3},{3,4},{4,5},{5,6},{6,7},{7,0},{8,9},{9,10},{10,1... | collective-permute-start | bytes 589832 | tf_op jit(solution)/shard_map/ppermute | solution.py:600
  195.8 7.7 %collective-permute-start.30 = (bf16[32,1536]{1,0:T(8,128)(2,1)S(1)}, bf16[32,1536]{1,0:T(8,128)(2,1)S(1)}, u32[]{:S(2)}, u32[]{:S(2)}) collective-permute-start(bf16[32,1536]{1,0:T(8,128)(2,1)S(1)} %slice.9), channel_id=1, source_target_pairs={{0,7},{1,0},{2,1},{3,2},{4,3},{5,4},{6,5},{7,6},{8,15},{9,8},{10,9... | collective-permute-start | bytes 294920 | tf_op jit(solution)/shard_map/ppermute | solution.py:601
  200.0 4.8 %collective-permute-start.29 = (bf16[32,1536]{1,0:T(8,128)(2,1)S(1)}, bf16[32,1536]{1,0:T(8,128)(2,1)S(1)}, u32[]{:S(2)}, u32[]{:S(2)}) collective-permute-start(bf16[32,1536]{1,0:T(8,128)(2,1)S(1)} %slice.8), channel_id=1, source_target_pairs={{0,1},{1,2},{2,3},{3,4},{4,5},{5,6},{6,7},{7,0},{8,9},{9,10},{10,1... | collective-permute-start | bytes 294920 | tf_op jit(solution)/shard_map/ppermute | solution.py:600
  (45 other events, 215.8 us)
